TPU v7x, 128 devices: a whole 4x4x4 slice. The times are simulated.
128 devices in a mesh: row: 8 (over y, z_lo), col: 16 (over z_hi, x, core).
Axes of the slice: x: 4, y: 4, z: 4 (z_hi: 2, z_lo: 2; z = z_hi * 2 + z_lo), core: 2. Of those that a mesh axis runs over, the one named last changes fastest.
Arguments:
- value: bfloat16 [1024, 1024, 128], P('row', 'col'), may hold values from -6 to 6
- gate: bfloat16 [1024, 1024, 128], P('row', 'col'), may hold values from -6 to 6
- filter_real: float32 [1024, 1024, 128], P(None, ('row', 'col')), may hold values from -6 to 6
- filter_imag: float32 [1024, 1024, 128], P(None, ('row', 'col')), may hold values from -6 to 6
- skip: float32 [128], replicated, may hold values from -4 to 4
Outputs:
- gated: bfloat16 [1024, 1024, 128], P('row', 'col')
All inputs are finite; a program needn't handle non-finite values.
Results may differ from a plain program's by a relative error of at most 0.001.
Values may be sent and summed in bfloat16 or wider, within the bound.
No kernel may reach another device: no remote copies, remote signals or barrier semaphores. Data moves between devices by JAX's collectives and lax.ppermute only.
A program may use at most 192 MiB of HBM per device.

v0:
```python
import math

import jax
import jax.numpy as jnp
from jax import lax
from jax.sharding import PartitionSpec as P

highest = lax.Precision.HIGHEST
full_turn = 2.0 * math.pi


def unit_roots(row_len, col_len, period, sign_value):
    left_iota = lax.broadcasted_iota(jnp.int32, (row_len, col_len), 0)
    right_iota = lax.broadcasted_iota(jnp.int32, (row_len, col_len), 1)
    phases = left_iota * right_iota % period
    angles = phases.astype(jnp.float32) * (sign_value * full_turn / period)
    return (jnp.cos(angles), jnp.sin(angles))


def rotation(row_len, col_len, period, sign_value):
    cosine, sine_part = unit_roots(row_len, col_len, period, sign_value)
    return jnp.stack([jnp.stack([cosine, -sine_part]), jnp.stack([sine_part, cosine])])


def rotate(complex_pair, cosine, sine_part):
    return jnp.stack(
        [
            complex_pair[0] * cosine - complex_pair[1] * sine_part,
            complex_pair[0] * sine_part + complex_pair[1] * cosine,
        ]
    )


def convolve(value, gate, filter_real, filter_imag, skip):
    row_count = lax.axis_size("row")
    col_count = lax.axis_size("col")
    local_rows, local_cols, channels = value.shape
    grid_rows = local_rows * row_count
    grid_cols = local_cols * col_count
    narrow = local_cols // row_count
    local_freq = grid_rows // (row_count * col_count)
    inner_len = min(128, grid_rows)
    outer_len = grid_rows // inner_len
    period = grid_rows * grid_cols
    pieces = value.reshape(local_rows, row_count, narrow, channels)
    columns = lax.all_to_all(pieces, "row", split_axis=1, concat_axis=0, tiled=True)
    real_part = columns.reshape(outer_len, inner_len, narrow, channels).astype(jnp.float32)
    first_matrix = rotation(outer_len, outer_len, outer_len, -1.0)[:, 0]
    interim = jnp.einsum("oku,uwjc->okwjc", first_matrix, real_part, precision=highest)
    row_cos, row_sin = unit_roots(outer_len, inner_len, grid_rows, -1.0)
    interim = rotate(interim, row_cos[:, :, None, None], row_sin[:, :, None, None])
    second_matrix = rotation(inner_len, inner_len, inner_len, -1.0)
    spectrum = jnp.einsum("oibw,ikwjc->obkjc", second_matrix, interim, precision=highest)
    spectrum = spectrum.reshape(2, grid_rows, narrow, channels)
    row_index = lax.axis_index("row")
    col_index = lax.axis_index("col")
    frequency = lax.broadcasted_iota(jnp.int32, (grid_rows, narrow), 0)
    position = (
        col_index * local_cols
        + row_index * narrow
        + lax.broadcasted_iota(jnp.int32, (grid_rows, narrow), 1)
    )
    phases = frequency * position % period
    angles = phases.astype(jnp.float32) * (-full_turn / period)
    twist_cos = jnp.cos(angles)[:, :, None]
    twist_sin = jnp.sin(angles)[:, :, None]
    spectrum = rotate(spectrum, twist_cos, twist_sin)
    arrived = lax.all_to_all(
        spectrum.reshape(2, grid_rows, 1, narrow, channels),
        ("row", "col"),
        split_axis=1,
        concat_axis=2,
        tiled=True,
    )
    arrived = arrived.reshape(2, local_freq, row_count, col_count, narrow, channels)
    col_matrix = rotation(col_count, col_count, col_count, -1.0)
    interim = jnp.einsum("oiac,iprcjz->oprajz", col_matrix, arrived, precision=highest)
    col_cos, col_sin = unit_roots(col_count, local_cols, grid_cols, -1.0)
    col_cos = jnp.transpose(col_cos.reshape(col_count, row_count, narrow), (1, 0, 2))
    col_sin = jnp.transpose(col_sin.reshape(col_count, row_count, narrow), (1, 0, 2))
    interim = rotate(interim, col_cos[None, :, :, :, None], col_sin[None, :, :, :, None])
    wide_matrix = rotation(local_cols, local_cols, local_cols, -1.0).reshape(
        2, 2, local_cols, row_count, narrow
    )
    frequencies = jnp.einsum("oibrj,iprajz->obapz", wide_matrix, interim, precision=highest)
    frequencies = frequencies.reshape(2, grid_cols, local_freq, channels)
    filtered = jnp.stack(
        [
            frequencies[0] * filter_real - frequencies[1] * filter_imag,
            frequencies[0] * filter_imag + frequencies[1] * filter_real,
        ]
    )
    filtered = filtered.reshape(2, local_cols, col_count, local_freq, channels)
    back_wide = rotation(local_cols, local_cols, local_cols, 1.0).reshape(
        2, 2, row_count, narrow, local_cols
    )
    interim = jnp.einsum("oirjb,ibapz->orjapz", back_wide, filtered, precision=highest)
    back_cos, back_sin = unit_roots(local_cols, col_count, grid_cols, 1.0)
    back_cos = back_cos.reshape(row_count, narrow, col_count)
    back_sin = back_sin.reshape(row_count, narrow, col_count)
    interim = rotate(interim, back_cos[:, :, :, None, None], back_sin[:, :, :, None, None])
    back_cols = rotation(col_count, col_count, col_count, 1.0)
    leaving = jnp.einsum("oica,irjapz->oprcjz", back_cols, interim, precision=highest)
    returned = lax.all_to_all(
        leaving.reshape(2, 1, local_freq, row_count * col_count, narrow, channels),
        ("row", "col"),
        split_axis=3,
        concat_axis=1,
        tiled=True,
    )
    returned = returned.reshape(2, grid_rows, narrow, channels)
    returned = rotate(returned, twist_cos, -twist_sin)
    returned = returned.reshape(2, inner_len, outer_len, narrow, channels)
    back_inner = rotation(inner_len, inner_len, inner_len, 1.0)
    interim = jnp.einsum("oinb,ibajz->onajz", back_inner, returned, precision=highest)
    inner_cos, inner_sin = unit_roots(inner_len, outer_len, grid_rows, 1.0)
    interim = rotate(interim, inner_cos[:, :, None, None], inner_sin[:, :, None, None])
    back_outer = rotation(outer_len, outer_len, outer_len, 1.0)[0]
    convolved = jnp.einsum("ima,inajz->mnjz", back_outer, interim, precision=highest)
    convolved = convolved.reshape(grid_rows, 1, narrow, channels) * (1.0 / period)
    settled = lax.all_to_all(convolved, "row", split_axis=0, concat_axis=1, tiled=True)
    settled = settled.reshape(local_rows, local_cols, channels)
    result = gate.astype(jnp.float32) * (settled + skip * value.astype(jnp.float32))
    return result.astype(jnp.bfloat16)


def shards(value, gate, filter_real, filter_imag, skip):
    return convolve(value, gate, filter_real, filter_imag, skip)


def solution(mesh):
    return jax.shard_map(
        shards,
        mesh=mesh,
        in_specs=(
            P("row", "col", None),
            P("row", "col", None),
            P(None, ("row", "col"), None),
            P(None, ("row", "col"), None),
            P(),
        ),
        out_specs=P("row", "col", None),
        check_vma=False,
    )
```

profile of v0, /device:TPU:66, one launch (start us, length us, event | category | flops | bytes accessed | tf_op | source)
XLA Modules:
  0.0 481.7 jit_solution(9626970155736999772)
XLA Ops:
  0.0 3.3 copy.111
  3.3 5.5 %all-to-all-start = ((bf16[128,8,8,128]{3,2,0,1:T(8,128)(2,1)}), bf16[128,8,8,128]{3,2,0,1:T(8,128)(2,1)S(1)}, u32[]{:S(2)}, u32[]{:S(2)}) async-start(bf16[128,8,8,128]{3,2,0,1:T(8,128)(2,1)} %copy.111), calls=%async_computation | async-start | bytes 4194304 | tf_op jit(solution)/shard_map/all_to_all | solution.py:46
  9.9 0.3 fusion.101
  10.2 0.3 multiply_sine_fusion
  10.5 29.5 %all-to-all-done = bf16[128,8,8,128]{3,2,0,1:T(8,128)(2,1)S(1)} async-done(((bf16[128,8,8,128]{3,2,0,1:T(8,128)(2,1)}), bf16[128,8,8,128]{3,2,0,1:T(8,128)(2,1)S(1)}, u32[]{:S(2)}, u32[]{:S(2)}) %all-to-all-start) | async-done | bytes 2097184 | tf_op jit(solution)/shard_map/all_to_all | solution.py:46
  40.0 3.8 fusion.37
  43.8 1.4 multiply_subtract_fusion.5
  45.2 1.7 pad_maximum_fusion
  46.8 13.2 %fusion.32 = f32[2,128,8,8,128]{4,1,3,2,0:T(8,128)S(1)} fusion(f32[2,8,128,8,128]{4,1,3,2,0:T(8,128)S(1)} %pad_maximum_fusion, f32[1,2,128,128]{3,2,1,0:T(8,128)S(1)} %get-tuple-element.26, f32[1,2,128,128]{3,2,1,0:T(8,128)S(1)} %get-tuple-element.25), kind=kOutput, calls=%fused_computation.54 | convolution fusion | flops 6442516480 | bytes 17039360 | tf_op jit(solution)/shard_map/oibw,ikwjc->obkjc/dot_general | solution.py:53
  60.0 1.1 fusion.156
  61.1 2.4 copy.116
  63.5 2.4 copy.118
  66.0 2.7 multiply_subtract_fusion.4
  68.7 0.5 maximum_bitcast_fusion
  69.3 3.9 copy.120
  73.2 7.9 %all-to-all-start.1 = ((f32[2,1024,1,8,128]{4,3,0,2,1:T(8,128)}), f32[2,1024,1,8,128]{4,3,0,2,1:T(8,128)}, u32[]{:S(2)}, u32[]{:S(2)}) async-start(f32[2,1024,1,8,128]{4,3,0,2,1:T(8,128)} %copy.120), calls=%async_computation.1 | async-start | bytes 16777216 | tf_op jit(solution)/shard_map/all_to_all | solution.py:68
  82.1 0.3 fusion.87
  82.4 97.4 %all-to-all-done.1 = f32[2,1024,1,8,128]{4,3,0,2,1:T(8,128)} async-done(((f32[2,1024,1,8,128]{4,3,0,2,1:T(8,128)}), f32[2,1024,1,8,128]{4,3,0,2,1:T(8,128)}, u32[]{:S(2)}, u32[]{:S(2)}) %all-to-all-start.1) | async-done | bytes 8388640 | tf_op jit(solution)/shard_map/all_to_all | solution.py:68
  179.8 3.9 copy.121
  183.7 12.9 %fusion.21 = f32[2,8,8,16,8,128]{5,3,0,4,2,1:T(8,128)S(1)} fusion(f32[2,8,8,16,8,128,1]{5,4,1,3,2,0,6:T(8,128)S(1)} %bitcast.182, f32[1,2,16,16]{3,2,1,0:T(8,128)S(1)} %get-tuple-element.30, f32[1,2,16,16]{3,2,1,0:T(8,128)S(1)} %get-tuple-element.29), kind=kOutput, calls=%fused_computation.49 | convolution fusion | flops 805307392 | bytes 16781312 | tf_op jit(solution)/shard_map/oiac,iprcjz->oprajz/dot_general | solution.py:77
  196.6 1.5 multiply_subtract_fusion.3
  198.1 0.9 maximum_bitcast_fusion.1
  198.9 13.3 %fusion.24 = f32[2,64,16,8,128]{4,1,0,2,3:T(8,128)S(1)} fusion(f32[2,8,8,16,8,128,1]{5,3,0,4,2,1,6:T(8,128)S(1)} %maximum_bitcast_fusion.1, f32[1,1,64,8,8]{2,3,4,1,0:T(8,128)S(1)} %get-tuple-element.40, f32[1,1,64,8,8]{2,3,4,1,0:T(8,128)S(1)} %get-tuple-element.39, f32[1,1,64,8,8]{2,3,4,1,0:T(8,128)S(1)} %get-tuple-element.38), kind=kOutput, calls=%fused_computation.50 | convolution fusion | flops 3221274624 | bytes 16826368 | tf_op jit(solution)/shard_map/oibrj,iprajz->obapz/dot_general | solution.py:85
  212.2 1.7 fusion.155
  213.9 2.4 copy.126
  216.3 4.4 copy.127
  220.7 8.8 %fusion.19 = (f32[1024,8,128]{2,1,0:T(8,128)}, f32[1024,8,128]{2,1,0:T(8,128)}) fusion(f32[1024,8,128]{2,1,0:T(8,128)} %param.8, f32[1,64,16,8,128]{4,3,2,1,0:T(8,128)} %copy.127, f32[1024,8,128]{2,1,0:T(8,128)} %param.7, f32[1,64,16,8,128]{4,3,2,1,0:T(8,128)S(1)} %copy.126), kind=kLoop, calls=%fused_computation.33 | loop fusion | flops 6291456 | bytes 25165824 | tf_op jit(solution)/shard_map/sub | solution.py:89
  229.5 4.8 copy.128
  234.3 2.6 copy.129
  237.0 8.5 %fusion.31 = f32[2,8,8,16,8,128]{5,2,4,3,1,0:T(8,128)S(1)} fusion(f32[1,64,16,8,128]{4,1,0,3,2:T(8,128)S(1)} %copy.129, f32[1,64,16,8,128]{4,1,0,3,2:T(8,128)S(1)} %copy.128, f32[1,1,8,8,64]{4,3,1,2,0:T(8,128)S(1)} %get-tuple-element.37, f32[1,1,8,8,64]{4,3,1,2,0:T(8,128)S(1)} %get-tuple-element.36, f32[1,1,8,8,64]{4,3,1,2,0:T(8,128)S(1)} %get-tuple-element.35), kind=kOutput, calls=%fused_computation.53 | convolution fusion | flops 3223371776 | bytes 16826368 | tf_op jit(solution)/shard_map/oirjb,ibapz->orjapz/dot_general | solution.py:97
  245.4 1.6 multiply_subtract_fusion.2
  247.0 1.7 maximum_bitcast_fusion.4
  248.7 13.4 %fusion.27 = f32[2,8,8,16,8,128]{5,3,0,1,4,2:T(8,128)S(1)} fusion(f32[2,8,8,16,8,128,1]{5,2,4,3,1,0,6:T(8,128)S(1)} %maximum_bitcast_fusion.4, f32[1,2,16,16]{3,2,1,0:T(8,128)S(1)} %get-tuple-element.28, f32[1,2,16,16]{3,2,1,0:T(8,128)S(1)} %get-tuple-element.27), kind=kOutput, calls=%fused_computation.51 | convolution fusion | flops 805307392 | bytes 16781312 | tf_op jit(solution)/shard_map/oica,irjapz->oprcjz/dot_general | solution.py:103
  262.1 4.9 %copy.132 = f32[2,8,8,16,8,128]{5,4,3,2,1,0:T(8,128)S(1)} copy(f32[2,8,8,16,8,128]{5,3,0,1,4,2:T(8,128)S(1)} %fusion.27) | data formatting | bytes 16777216 | tf_op jit(solution)/shard_map/oica,irjapz->oprcjz/transpose | solution.py:103
  266.9 4.4 copy.133
  271.4 14.4 %all-to-all-start.2 = ((f32[2,1,8,128,8,128]{5,4,2,0,1,3:T(8,128)}), f32[2,1,8,128,8,128]{5,4,2,0,1,3:T(8,128)}, u32[]{:S(2)}, u32[]{:S(2)}) async-start(f32[2,1,8,128,8,128]{5,4,2,0,1,3:T(8,128)} %copy.133), calls=%async_computation.2 | async-start | bytes 16777216 | tf_op jit(solution)/shard_map/all_to_all | solution.py:104
  285.9 0.3 fusion.100
  286.2 0.3 multiply_sine_fusion.1
  286.7 97.9 %all-to-all-done.2 = f32[2,1,8,128,8,128]{5,4,2,0,1,3:T(8,128)} async-done(((f32[2,1,8,128,8,128]{5,4,2,0,1,3:T(8,128)}), f32[2,1,8,128,8,128]{5,4,2,0,1,3:T(8,128)}, u32[]{:S(2)}, u32[]{:S(2)}) %all-to-all-start.2) | async-done | bytes 8388640 | tf_op jit(solution)/shard_map/all_to_all | solution.py:104
  384.7 8.2 %copy.196 = f32[2,1,8,128,8,128]{5,3,4,2,0,1:T(8,128)S(1)} copy(f32[2,1,8,128,8,128]{5,4,2,0,1,3:T(8,128)} %all-to-all-done.2) | data formatting | bytes 16777216 | tf_op jit(solution)/shard_map/all_to_all | solution.py:104
  392.9 3.0 multiply_subtract_fusion.1
  395.9 7.7 %fusion.30 = f32[2,128,8,8,128]{4,1,3,2,0:T(8,128)S(1)} fusion(f32[1,128,8,8,128]{4,1,0,3,2:T(8,128)S(1)} %get-tuple-element.14, f32[1,128,8,8,128]{4,1,0,3,2:T(8,128)S(1)} %get-tuple-element.13, f32[1,2,128,128]{3,2,1,0:T(8,128)S(1)} %get-tuple-element.24, f32[1,2,128,128]{3,2,1,0:T(8,128)S(1)} %get-tuple-element.23), kind=kOutput, calls=%fused_computation.52 | convolution fusion | flops 6444613632 | bytes 17039360 | tf_op jit(solution)/shard_map/oinb,ibajz->onajz/dot_general | solution.py:115
  403.6 1.8 multiply_subtract_fusion
  405.5 1.1 pad_maximum_fusion.1
  406.6 11.8 %bitcast_multiply_fusion = f32[8,128,8,128]{3,0,2,1:T(8,128)S(1)} fusion(f32[2,128,8,8,128]{4,1,3,2,0:T(8,128)S(1)} %pad_maximum_fusion.1, f32[1,8,8]{2,1,0:T(8,128)S(1)} %get-tuple-element.59, f32[1,8,8]{2,1,0:T(8,128)S(1)} %get-tuple-element.60), kind=kOutput, calls=%fused_computation.30 | convolution fusion | flops 202375296 | bytes 12583424 | tf_op jit(solution)/shard_map/ima,inajz->mnjz/dot_general | solution.py:119
  418.4 0.8 copy.138
  419.2 59.9 %all_to_all.60 = f32[1024,1,8,128]{3,2,1,0:T(8,128)S(1)} all-to-all(f32[1024,1,8,128]{3,2,1,0:T(8,128)S(1)} %bitcast.186), channel_id=1, replica_groups=mesh['row'=8,'col'=16] {'row'}, dimensions={0} | all-to-all | bytes 8388608 | tf_op jit(solution)/shard_map/all_to_all | solution.py:121
  479.1 2.4 fusion.18
  (40 shorter events, 2.4 us)
Async XLA Ops:
  3.3 36.7 %all-to-all-start = ((bf16[128,8,8,128]{3,2,0,1:T(8,128)(2,1)}), bf16[128,8,8,128]{3,2,0,1:T(8,128)(2,1)S(1)}, u32[]{:S(2)}, u32[]{:S(2)}) async-start(bf16[128,8,8,128]{3,2,0,1:T(8,128)(2,1)} %copy.111), calls=%async_computation | async-start | bytes 4194304 | tf_op jit(solution)/shard_map/all_to_all | solution.py:46
  9.2 1.3 copy-start.3
  73.2 106.6 %all-to-all-start.1 = ((f32[2,1024,1,8,128]{4,3,0,2,1:T(8,128)}), f32[2,1024,1,8,128]{4,3,0,2,1:T(8,128)}, u32[]{:S(2)}, u32[]{:S(2)}) async-start(f32[2,1024,1,8,128]{4,3,0,2,1:T(8,128)} %copy.120), calls=%async_computation.1 | async-start | bytes 16777216 | tf_op jit(solution)/shard_map/all_to_all | solution.py:68
  229.5 4.8 copy-start
  271.4 15.1 %copy-start.4 = (s32[8]{0:T(128)S(1)}, s32[8]{0:T(128)}, u32[]{:S(2)}) copy-start(s32[8]{0:T(128)} %copy-done.3) | copy-start | bytes 100
  271.4 113.3 %all-to-all-start.2 = ((f32[2,1,8,128,8,128]{5,4,2,0,1,3:T(8,128)}), f32[2,1,8,128,8,128]{5,4,2,0,1,3:T(8,128)}, u32[]{:S(2)}, u32[]{:S(2)}) async-start(f32[2,1,8,128,8,128]{5,4,2,0,1,3:T(8,128)} %copy.133), calls=%async_computation.2 | async-start | bytes 16777216 | tf_op jit(solution)/shard_map/all_to_all | solution.py:104
  419.2 60.0 %copy-start.1 = (bf16[128,64,128]{2,1,0:T(8,128)(2,1)S(1)}, bf16[128,64,128]{2,1,0:T(8,128)(2,1)}, u32[]{:S(2)}) copy-start(bf16[128,64,128]{2,1,0:T(8,128)(2,1)} %param.5) | copy-start | bytes 6291460
  419.2 59.9 %copy-start.2 = (bf16[128,64,128]{2,1,0:T(8,128)(2,1)S(1)}, bf16[128,64,128]{2,1,0:T(8,128)(2,1)}, u32[]{:S(2)}) copy-start(bf16[128,64,128]{2,1,0:T(8,128)(2,1)} %param.6) | copy-start | bytes 6291460
  419.2 59.9 %copy-start.5 = (f32[128]{0:T(128)S(1)}, f32[128]{0:T(128)}, u32[]{:S(2)}) copy-start(f32[128]{0:T(128)} %param.9) | copy-start | bytes 1540
where the time goes:
time: 487 us; the launch traced here: 482 us
  waiting for transfers between devices  225 us (46%)
  matrix products  84.5 us (17%)
  blocking collectives  59.9 us (12%)
  local copies, waits for them, and re-layouts  52 us (11%)
  other arithmetic  32 us (7%)
  starting transfers between devices  27.8 us (6%)
    all_to_all x1, waiting for transfers between devices, convolve(): lax.all_to_all(leaving.reshape(2, 1, local_freq, row_count * col_count, n...  97.9 us
    all_to_all x1, waiting for transfers between devices, convolve(): lax.all_to_all(spectrum.reshape(2, grid_rows, 1, narrow, channels), ('row...  97.4 us
    all_to_all x1, blocking collectives, convolve(): lax.all_to_all(convolved, 'row', split_axis=0, concat_axis=1, tiled=True)  59.9 us
    all_to_all x1, waiting for transfers between devices, convolve(): lax.all_to_all(pieces, 'row', split_axis=1, concat_axis=0, tiled=True)  29.5 us
    all_to_all x1, starting transfers between devices, convolve(): lax.all_to_all(leaving.reshape(2, 1, local_freq, row_count * col_count, n...  14.4 us
    dot_general x1, matrix products, convolve(): jnp.einsum('oica,irjapz->oprcjz', back_cols, interim, precision=highest)  13.4 us
    dot_general x1, matrix products, convolve(): jnp.einsum('oibrj,iprajz->obapz', wide_matrix, interim, precision=highest)  13.3 us
    dot_general x1, matrix products, convolve(): jnp.einsum('oibw,ikwjc->obkjc', second_matrix, interim, precision=highest)  13.2 us
  transfers between devices with their start and end apart: 3, of which 3 were waited for; matrix products, arithmetic and copies ran while one was open for 1% of the time, Pallas kernels for 0%

commit v1 on v0

v1 whole, which is shorter than its diff:
```python
import math

import jax
import jax.numpy as jnp
import numpy as np
from jax import lax
from jax.experimental import pallas as pl
from jax.experimental.pallas import tpu as pltpu
from jax.sharding import PartitionSpec as P

half_root = math.sqrt(0.5)
span = 124.0
ln2 = math.log(2.0)
f32 = jnp.float32
bf16 = jnp.bfloat16
vmem_bytes = 56 * 1024 * 1024


def turn(x, sign):
    re, im = x
    return (-im, re) if sign > 0 else (im, -re)


def add(x, y):
    return (x[0] + y[0], x[1] + y[1])


def sub(x, y):
    return (x[0] - y[0], x[1] - y[1])


def scale_root(x, index, period, sign):
    index %= period
    if index == 0:
        return x
    if 4 * index == period:
        return turn(x, sign)
    if 2 * index == period:
        return (-x[0], -x[1])
    re, im = x
    if 8 * index == period:
        if sign > 0:
            return ((re - im) * half_root, (im + re) * half_root)
        return ((re + im) * half_root, (im - re) * half_root)
    if 8 * index == 3 * period:
        if sign > 0:
            return ((re + im) * -half_root, (re - im) * half_root)
        return ((im - re) * half_root, (re + im) * -half_root)
    angle = 2.0 * math.pi * index / period
    c, s = math.cos(angle), sign * math.sin(angle)
    return (re * c - im * s, re * s + im * c)


def times(x, c, s):
    re, im = x
    return (re * c - im * s, re * s + im * c)


def times_conj(x, c, s):
    re, im = x
    return (re * c + im * s, im * c - re * s)


def dft4(y, sign):
    t0, t1 = add(y[0], y[2]), sub(y[0], y[2])
    t2, t3 = add(y[1], y[3]), turn(sub(y[1], y[3]), sign)
    return [add(t0, t2), add(t1, t3), sub(t0, t2), sub(t1, t3)]


def dft8(x, sign):
    even = dft4([add(x[k], x[k + 4]) for k in range(4)], sign)
    odd = dft4([scale_root(sub(x[k], x[k + 4]), k, 8, sign) for k in range(4)], sign)
    return [even[0], odd[0], even[1], odd[1], even[2], odd[2], even[3], odd[3]]


def dft16(x, sign):
    first = [dft4([x[4 * a + b] for a in range(4)], sign) for b in range(4)]
    out = [None] * 16
    for c in range(4):
        last = dft4([scale_root(first[b][c], b * c, 16, sign) for b in range(4)], sign)
        for e in range(4):
            out[c + 4 * e] = last[e]
    return out


def get(re_ref, im_ref, i, at):
    return (re_ref[i, at], im_ref[i, at])


def put(re_ref, im_ref, i, at, x):
    re_ref[i, at] = x[0]
    im_ref[i, at] = x[1]


def transform_128(re_ref, im_ref, i, sign):
    for b in range(16):
        x = dft8([get(re_ref, im_ref, i, 16 * a + b) for a in range(8)], sign)
        for c in range(8):
            put(re_ref, im_ref, i, 16 * c + b, scale_root(x[c], b * c, 128, sign))
    for c in range(8):
        x = dft16([get(re_ref, im_ref, i, 16 * c + b) for b in range(16)], sign)
        for e in range(16):
            put(re_ref, im_ref, i, 16 * c + e, x[e])


def untransform_128(re_ref, im_ref, i, sign):
    for c in range(8):
        x = dft16([get(re_ref, im_ref, i, 16 * c + e) for e in range(16)], sign)
        for b in range(16):
            put(re_ref, im_ref, i, 16 * c + b, scale_root(x[b], b * c, 128, sign))
    for b in range(16):
        x = dft8([get(re_ref, im_ref, i, 16 * c + b) for c in range(8)], sign)
        for a in range(8):
            put(re_ref, im_ref, i, 16 * a + b, x[a])


def place(k):
    return 16 * (k % 8) + k // 8


def encode(blocks, store):
    top = jnp.abs(blocks[0])
    for x in blocks[1:]:
        top = jnp.maximum(top, jnp.abs(x))
    scale = jnp.maximum(top * (1.0 / span), 1e-35).astype(bf16)
    inverse = 1.0 / scale.astype(f32)
    for k in range(8):
        pair = jnp.concatenate([blocks[2 * k] * inverse, blocks[2 * k + 1] * inverse], axis=0)
        store(slice(16 * k, 16 * k + 16), jnp.exp2(pair).astype(bf16))
    store(slice(128, 136), scale)


def decode_scale(rows):
    return rows.astype(f32) * (1.0 / ln2)


def decode_pair(rows):
    logs = jnp.log(rows.astype(f32))
    return logs[0:8], logs[8:16]


def forward_kernel(x_ref, table_ref, out_ref, re_ref, im_ref):
    def first(pair, carry):
        both = [x_ref[64 * r + pair].astype(f32) for r in range(8)]
        for odd in range(2):
            m = 2 * pair + odd
            x = [v[8 * odd : 8 * odd + 8] for v in both]
            s = [x[k] + x[k + 4] for k in range(4)]
            d = [x[k] - x[k + 4] for k in range(4)]
            s02, s13 = s[0] + s[2], s[1] + s[3]
            re_ref[0, m] = s02 + s13
            im_ref[0, m] = jnp.zeros_like(s02)
            low, high = (d[1] - d[3]) * half_root, (d[1] + d[3]) * half_root
            rows = [None, (d[0] + low, -d[2] - high), (s[0] - s[2], s[3] - s[1]), (d[0] - low, d[2] - high)]
            for i in range(1, 4):
                put(re_ref, im_ref, i, m, times(rows[i], table_ref[16 * m + i], table_ref[16 * m + 8 + i]))
            mid = s02 - s13
            put(re_ref, im_ref, 4, m, (mid * table_ref[16 * m + 4], mid * table_ref[16 * m + 12]))
        return carry

    lax.fori_loop(0, 64, first, 0)

    def second(i, carry):
        transform_128(re_ref, im_ref, i, -1)
        return carry

    lax.fori_loop(0, 5, second, 0)

    def third(d, carry):
        here, there = place(d), place(127 - d)
        blocks = []
        for i in range(5):
            blocks += [re_ref[i, here], im_ref[i, here]]
        for i in range(5, 8):
            blocks += [re_ref[8 - i, there], -im_ref[8 - i, there]]

        def store(rows, v):
            out_ref[d, rows, :] = v

        encode(blocks, store)
        return carry

    lax.fori_loop(0, 128, third, 0)


def middle_kernel(x_ref, twist_cos, twist_sin, filter_real, filter_imag, table_ref, out_ref,
                  re_ref, im_ref, tc_ref, ts_ref, fr_ref, fi_ref, sems):
    copies = [
        pltpu.make_async_copy(src, dst, sems.at[k])
        for k, (src, dst) in enumerate(
            [(twist_cos, tc_ref), (twist_sin, ts_ref), (filter_real, fr_ref), (filter_imag, fi_ref)]
        )
    ]
    for c in copies:
        c.start()
    copies[0].wait()
    copies[1].wait()

    def first(src, carry):
        a = 8 * (src % 16) + src // 16
        scale = decode_scale(x_ref[src, 128:136, :])
        for i in range(8):
            x = decode_pair(x_ref[src, 16 * i : 16 * i + 16, :])
            y = times(x, scale * tc_ref[a, i], scale * ts_ref[a, i])
            put(re_ref, im_ref, i, a, y)
        return carry

    lax.fori_loop(0, 128, first, 0)

    def second(i, carry):
        transform_128(re_ref, im_ref, i, -1)
        return carry

    lax.fori_loop(0, 8, second, 0)
    copies[2].wait()
    copies[3].wait()

    def third(at, carry):
        b = at // 16 + 8 * (at % 16)
        re = jnp.stack([re_ref[i, at] for i in range(8)])
        im = jnp.stack([im_ref[i, at] for i in range(8)])
        re, im = jnp.swapaxes(re, 0, 1), jnp.swapaxes(im, 0, 1)
        x = [(re[0], im[0])]
        for j in range(1, 8):
            x.append(times((re[j], im[j]), table_ref[16 * b + j], table_ref[16 * b + 8 + j]))
        x = dft8(x, -1)
        y = [times(x[e], fr_ref[b + 128 * e], fi_ref[b + 128 * e]) for e in range(8)]
        y = dft8(y, 1)
        for j in range(1, 8):
            y[j] = times_conj(y[j], table_ref[16 * b + j], table_ref[16 * b + 8 + j])
        re = jnp.swapaxes(jnp.stack([v[0] for v in y]), 0, 1)
        im = jnp.swapaxes(jnp.stack([v[1] for v in y]), 0, 1)
        for i in range(8):
            put(re_ref, im_ref, i, at, (re[i], im[i]))
        return carry

    lax.fori_loop(0, 128, third, 0)

    def fourth(i, carry):
        untransform_128(re_ref, im_ref, i, 1)
        return carry

    lax.fori_loop(0, 8, fourth, 0)

    def fifth(src, carry):
        a = 8 * (src % 16) + src // 16
        blocks = []
        for i in range(8):
            blocks += times_conj(get(re_ref, im_ref, i, a), tc_ref[a, i], ts_ref[a, i])

        def store(rows, v):
            out_ref[src, rows, :] = v

        encode(blocks, store)
        return carry

    lax.fori_loop(0, 128, fifth, 0)


def backward_kernel(x_ref, table_ref, out_ref, re_ref, im_ref, conv_ref):
    def first(d, carry):
        sides = []
        for src in (d, 127 - d):
            scale = decode_scale(x_ref[src, 128:136, :])
            side = []
            for i in range(8):
                lre, lim = decode_pair(x_ref[src, 16 * i : 16 * i + 16, :])
                side.append((lre * scale, lim * scale))
            sides.append(side)
        for k, src in enumerate((d, 127 - d)):
            near, far = sides[k], sides[1 - k]
            put(re_ref, im_ref, 0, src, near[0])
            put(re_ref, im_ref, 4, src, near[4])
            for i in range(1, 4):
                put(re_ref, im_ref, i, src, (near[i][0] + far[8 - i][0], near[i][1] - far[8 - i][1]))
        return carry

    lax.fori_loop(0, 64, first, 0)

    def second(i, carry):
        transform_128(re_ref, im_ref, i, 1)
        return carry

    lax.fori_loop(0, 5, second, 0)

    def third(at, carry):
        m = at // 16 + 8 * (at % 16)
        u0 = re_ref[0, at]
        z = [times_conj(get(re_ref, im_ref, i, at), table_ref[16 * m + i], table_ref[16 * m + 8 + i]) for i in range(1, 4)]
        re4, im4 = get(re_ref, im_ref, 4, at)
        u4 = re4 * table_ref[16 * m + 4] + im4 * table_ref[16 * m + 12]
        (x1, y1), (x2, y2), (x3, y3) = z
        even, odd = u0 + u4, u0 - u4
        x13, y13 = x1 + x3, y1 - y3
        up, down = even + x2, even - x2
        conv_ref[0, m] = up + x13
        conv_ref[4, m] = up - x13
        conv_ref[2, m] = down - y13
        conv_ref[6, m] = down + y13
        aa, bb = (x1 - x3) * half_root, (y1 + y3) * half_root
        up, down = odd + y2, odd - y2
        diff, both = aa - bb, aa + bb
        conv_ref[1, m] = down + diff
        conv_ref[5, m] = down - diff
        conv_ref[3, m] = up - both
        conv_ref[7, m] = up + both
        return carry

    lax.fori_loop(0, 128, third, 0)

    def fourth(step, carry):
        r, g = step // 8, step % 8
        blocks = [conv_ref[r, 16 * g + k] * (1.0 / 1048576.0) for k in range(16)]

        def store(rows, v):
            out_ref[r, g, rows, :] = v

        encode(blocks, store)
        return carry

    lax.fori_loop(0, 64, fourth, 0)


def gate_kernel(x_ref, value_ref, gate_ref, skip_ref, out_ref):
    skip = skip_ref[0:1, :]

    def body(k, carry):
        start = pl.multiple_of(16 * k, 16)
        for pair in range(4):
            sides = []
            for r in (2 * pair, 2 * pair + 1):
                scale = decode_scale(x_ref[r, 0, 128:136, :])
                low, high = decode_pair(x_ref[r, 0, pl.ds(start, 16), :])
                sides.append((low * scale, high * scale))
            for odd in range(2):
                conv = jnp.concatenate([sides[0][odd], sides[1][odd]], axis=0)
                rows = slice(16 * pair, 16 * pair + 16)
                v = value_ref[2 * k + odd, rows, :].astype(f32)
                g = gate_ref[2 * k + odd, rows, :].astype(f32)
                out_ref[2 * k + odd, rows, :] = (g * (conv + skip * v)).astype(bf16)
        return carry

    lax.fori_loop(0, 8, body, 0)


def roots_table(period):
    m, i = np.arange(128)[:, None], np.arange(8)[None, :]
    angle = -2.0 * np.pi * (m * i % period) / period
    return np.concatenate([np.cos(angle), np.sin(angle)], axis=1).astype(np.float32).reshape(-1)


def twist_tables(device):
    shape = (128, 8, 8)
    q = 8 * lax.broadcasted_iota(jnp.int32, shape, 0) + lax.broadcasted_iota(jnp.int32, shape, 2)
    kp = 8 * device + lax.broadcasted_iota(jnp.int32, shape, 1)
    angle = (q * kp % 1048576).astype(f32) * (-2.0 * math.pi / 1048576.0)
    cosine, sine = lax.optimization_barrier((jnp.cos(angle), jnp.sin(angle)))
    wide = shape + (128,)
    return jnp.broadcast_to(cosine[..., None], wide), jnp.broadcast_to(sine[..., None], wide)


def vspec():
    return pl.BlockSpec(memory_space=pltpu.VMEM)


def sspec():
    return pl.BlockSpec(memory_space=pltpu.SMEM)


def aspec():
    return pl.BlockSpec(memory_space=pl.ANY)


def params():
    return pltpu.CompilerParams(vmem_limit_bytes=vmem_bytes)


def forward(columns, table):
    return pl.pallas_call(
        forward_kernel,
        out_shape=jax.ShapeDtypeStruct((128, 136, 128), bf16),
        in_specs=[vspec(), sspec()],
        out_specs=vspec(),
        scratch_shapes=[pltpu.VMEM((5, 128, 8, 128), f32)] * 2,
        compiler_params=params(),
        name="forward_columns",
    )(columns, table)


def middle(arrived, twist_cos, twist_sin, filter_real, filter_imag, table):
    return pl.pallas_call(
        middle_kernel,
        out_shape=jax.ShapeDtypeStruct((128, 136, 128), bf16),
        in_specs=[vspec()] + [aspec()] * 4 + [sspec()],
        out_specs=vspec(),
        scratch_shapes=[pltpu.VMEM((8, 128, 8, 128), f32)] * 2
        + [pltpu.VMEM((128, 8, 8, 128), f32)] * 2
        + [pltpu.VMEM((1024, 8, 128), f32)] * 2
        + [pltpu.SemaphoreType.DMA((4,))],
        compiler_params=params(),
        name="filter_rows",
    )(arrived, twist_cos, twist_sin, filter_real, filter_imag, table)


def backward(returned, table):
    return pl.pallas_call(
        backward_kernel,
        out_shape=jax.ShapeDtypeStruct((8, 8, 136, 128), bf16),
        in_specs=[vspec(), sspec()],
        out_specs=vspec(),
        scratch_shapes=[pltpu.VMEM((5, 128, 8, 128), f32)] * 2 + [pltpu.VMEM((8, 128, 8, 128), f32)],
        compiler_params=params(),
        name="backward_columns",
    )(returned, table)


def gating(settled, value, gate, skip):
    return pl.pallas_call(
        gate_kernel,
        grid=(8,),
        out_shape=jax.ShapeDtypeStruct((128, 64, 128), bf16),
        in_specs=[
            pl.BlockSpec((8, 1, 136, 128), lambda g: (0, g, 0, 0)),
            pl.BlockSpec((16, 64, 128), lambda g: (g, 0, 0)),
            pl.BlockSpec((16, 64, 128), lambda g: (g, 0, 0)),
            pl.BlockSpec((1, 128), lambda g: (0, 0)),
        ],
        out_specs=pl.BlockSpec((16, 64, 128), lambda g: (g, 0, 0)),
        compiler_params=params(),
        name="gating",
    )(settled, value, gate, skip.reshape(1, 128))


def convolve(value, gate, filter_real, filter_imag, skip):
    device = lax.axis_index("row") * 16 + lax.axis_index("col")
    table = jnp.asarray(roots_table(1024))
    pieces = value.reshape(128, 8, 8, 128)
    columns = lax.all_to_all(pieces, "row", split_axis=1, concat_axis=0, tiled=True)
    spectrum = forward(columns.reshape(512, 16, 128), table)
    twist_cos, twist_sin = twist_tables(device)
    arrived = lax.all_to_all(spectrum, ("row", "col"), split_axis=0, concat_axis=0, tiled=True)
    leaving = middle(arrived, twist_cos, twist_sin, filter_real, filter_imag, table)
    returned = lax.all_to_all(leaving, ("row", "col"), split_axis=0, concat_axis=0, tiled=True)
    convolved = backward(returned, table)
    settled = lax.all_to_all(convolved, "row", split_axis=0, concat_axis=0, tiled=True)
    return gating(settled, value, gate, skip)


def solution(mesh):
    return jax.shard_map(
        convolve,
        mesh=mesh,
        in_specs=(
            P("row", "col", None),
            P("row", "col", None),
            P(None, ("row", "col"), None),
            P(None, ("row", "col"), None),
            P(),
        ),
        out_specs=P("row", "col", None),
        check_vma=False,
    )
```

time: 487 us -> 265 us (0.54)
  the two profiles are of different devices: /device:TPU:66 before, /device:TPU:0 now
where the time goes in v1:
time: 265 us; the launch traced here: 264 us
  blocking collectives  127 us (48%)
  Pallas kernels  65.1 us (25%)
  waiting for transfers between devices  53.1 us (20%)
  starting transfers between devices  9.6 us (4%)
  local copies, waits for them, and re-layouts  7.11 us (3%)
    all_to_all x1, blocking collectives, convolve(): lax.all_to_all(leaving, ('row', 'col'), split_axis=0, concat_axis=0, tile...  61.3 us
    all_to_all x1, waiting for transfers between devices, convolve(): lax.all_to_all(spectrum, ('row', 'col'), split_axis=0, concat_axis=0, til...  53.1 us
    all_to_all x1, blocking collectives, convolve(): lax.all_to_all(convolved, 'row', split_axis=0, concat_axis=0, tiled=True)  33 us
    pallas_call x1, Pallas kernels, middle(): pl.pallas_call(middle_kernel, out_shape=jax.ShapeDtypeStruct((128, 136, 1...  32.5 us
    all_to_all x1, blocking collectives, convolve(): lax.all_to_all(pieces, 'row', split_axis=1, concat_axis=0, tiled=True)  32.4 us
    pallas_call x1, Pallas kernels, backward(): pl.pallas_call(backward_kernel, out_shape=jax.ShapeDtypeStruct((8, 8, 136...  12.7 us
    pallas_call x1, Pallas kernels, forward(): pl.pallas_call(forward_kernel, out_shape=jax.ShapeDtypeStruct((128, 136,...  12.5 us
    all_to_all x1, starting transfers between devices, convolve(): lax.all_to_all(spectrum, ('row', 'col'), split_axis=0, concat_axis=0, til...  9.6 us
  transfers between devices with their start and end apart: 1, of which 1 were waited for; matrix products, arithmetic and copies ran while one was open for 1% of the time, Pallas kernels for 0%

profile of v1, /device:TPU:0, one launch (start us, length us, event | category | flops | bytes accessed | tf_op | source)
XLA Modules:
  0.0 263.9 jit_solution(11812205505615305352)
XLA Ops:
  0.0 2.0 copy.7
  2.0 32.4 %all_to_all.30 = bf16[128,8,8,128]{3,2,0,1:T(8,128)(2,1)} all-to-all(bf16[128,8,8,128]{3,2,0,1:T(8,128)(2,1)S(1)} %copy.7), channel_id=1, replica_groups=mesh['row'=8,'col'=16] {'row'}, dimensions={1} | all-to-all | bytes 4194304 | tf_op jit(solution)/shard_map/all_to_all | solution.py:438
  34.4 12.5 %forward_columns.1 = bf16[128,136,128]{2,1,0:T(8,128)(2,1)} custom-call(bf16[512,16,128]{2,1,0:T(8,128)(2,1)} %bitcast.7, f32[2048]{0:T(1024)} %constant.33.clone.table_ref), custom_call_target="tpu_custom_call" | custom-call | tf_op jit(solution)/shard_map/forward_columns/pallas_call | solution.py:379
  46.9 9.6 %all-to-all-start.1 = ((bf16[128,136,128]{2,1,0:T(8,128)(2,1)}), bf16[128,136,128]{2,1,0:T(8,128)(2,1)}, u32[]{:S(2)}, u32[]{:S(2)}) async-start(bf16[128,136,128]{2,1,0:T(8,128)(2,1)} %forward_columns.1), calls=%async_computation.1 | async-start | bytes 8912896 | tf_op jit(solution)/shard_map/all_to_all | solution.py:441
  56.6 2.1 fusion.3
  58.7 53.1 %all-to-all-done.1.x_ref = bf16[128,136,128]{2,1,0:T(8,128)(2,1)} async-done(((bf16[128,136,128]{2,1,0:T(8,128)(2,1)}), bf16[128,136,128]{2,1,0:T(8,128)(2,1)}, u32[]{:S(2)}, u32[]{:S(2)}) %all-to-all-start.1) | async-done | bytes 4456480 | tf_op jit(solution)/shard_map/all_to_all | solution.py:441
  111.8 2.6 broadcast_in_dim.4.twist_cos
  114.4 2.5 broadcast_in_dim.5.twist_sin
  117.0 32.5 %filter_rows.1 = bf16[128,136,128]{2,1,0:T(8,128)(2,1)} custom-call(bf16[128,136,128]{2,1,0:T(8,128)(2,1)} %all-to-all-done.1.x_ref, f32[128,8,8,128]{3,2,1,0:T(8,128)} %broadcast_in_dim.4.twist_cos, f32[128,8,8,128]{3,2,1,0:T(8,128)} %broadcast_in_dim.5.twist_sin, f32[1024,8,128]{2,1,0:T(8,128)} %filter_real.1, f32[1024,8,128]{2,1,0:T(8,128)} %filter_imag.1, ...), custom_call_target="tpu_custom_call" | custom-call | tf_op jit(solution)/shard_map/filter_rows/pallas_call | solution.py:391
  149.5 61.3 %all_to_all.31.x_ref = bf16[128,136,128]{2,1,0:T(8,128)(2,1)} all-to-all(bf16[128,136,128]{2,1,0:T(8,128)(2,1)} %filter_rows.1), channel_id=1, replica_groups=mesh['row'=8,'col'=16] {'row','col'}, dimensions={0} | all-to-all | bytes 8912896 | tf_op jit(solution)/shard_map/all_to_all | solution.py:443
  210.8 12.7 %backward_columns.1 = bf16[8,8,136,128]{3,2,1,0:T(8,128)(2,1)} custom-call(bf16[128,136,128]{2,1,0:T(8,128)(2,1)} %all_to_all.31.x_ref, f32[2048]{0:T(1024)} %constant.33.clone.table_ref), custom_call_target="tpu_custom_call" | custom-call | tf_op jit(solution)/shard_map/backward_columns/pallas_call | solution.py:406
  223.5 33.0 %all_to_all.32.x_ref = bf16[8,8,136,128]{3,2,1,0:T(8,128)(2,1)} all-to-all(bf16[8,8,136,128]{3,2,1,0:T(8,128)(2,1)} %backward_columns.1), channel_id=1, replica_groups=mesh['row'=8,'col'=16] {'row'}, dimensions={0} | all-to-all | bytes 4456448 | tf_op jit(solution)/shard_map/all_to_all | solution.py:445
  256.5 7.4 %gating.1 = bf16[128,64,128]{2,1,0:T(8,128)(2,1)} custom-call(bf16[8,8,136,128]{3,2,1,0:T(8,128)(2,1)} %all_to_all.32.x_ref, bf16[128,64,128]{2,1,0:T(8,128)(2,1)} %value_ref.1, bf16[128,64,128]{2,1,0:T(8,128)(2,1)} %gate_ref.1, f32[1,128]{1,0:T(1,128)} %bitcast.9), custom_call_target="tpu_custom_call" | custom-call | tf_op jit(solution)/shard_map/gating/pallas_call | solution.py:418
  (2 shorter events, 0.0 us)
Async XLA Ops:
  46.9 64.9 %all-to-all-start.1 = ((bf16[128,136,128]{2,1,0:T(8,128)(2,1)}), bf16[128,136,128]{2,1,0:T(8,128)(2,1)}, u32[]{:S(2)}, u32[]{:S(2)}) async-start(bf16[128,136,128]{2,1,0:T(8,128)(2,1)} %forward_columns.1), calls=%async_computation.1 | async-start | bytes 8912896 | tf_op jit(solution)/shard_map/all_to_all | solution.py:441

commit v2 on v1

v2 whole, which is shorter than its diff:
```python
import math

import jax
import jax.numpy as jnp
import numpy as np
from jax import lax
from jax.experimental import pallas as pl
from jax.experimental.pallas import tpu as pltpu
from jax.sharding import PartitionSpec as P

TM = 4
TE = 8
TD = 8
half_root = math.sqrt(0.5)
span = 124.0
ln2 = math.log(2.0)
f32 = jnp.float32
bf16 = jnp.bfloat16


def turn(x, sign):
    re, im = x
    return (-im, re) if sign > 0 else (im, -re)


def add(x, y):
    return (x[0] + y[0], x[1] + y[1])


def sub(x, y):
    return (x[0] - y[0], x[1] - y[1])


def scale_root(x, index, period, sign):
    index %= period
    if index == 0:
        return x
    if 4 * index == period:
        return turn(x, sign)
    if 2 * index == period:
        return (-x[0], -x[1])
    re, im = x
    if 8 * index == period:
        if sign > 0:
            return ((re - im) * half_root, (im + re) * half_root)
        return ((re + im) * half_root, (im - re) * half_root)
    if 8 * index == 3 * period:
        if sign > 0:
            return ((re + im) * -half_root, (re - im) * half_root)
        return ((im - re) * half_root, (re + im) * -half_root)
    angle = 2.0 * math.pi * index / period
    c, s = math.cos(angle), sign * math.sin(angle)
    return (re * c - im * s, re * s + im * c)


def times(x, c, s):
    re, im = x
    return (re * c - im * s, re * s + im * c)


def times_conj(x, c, s):
    re, im = x
    return (re * c + im * s, im * c - re * s)


def dft4(y, sign):
    t0, t1 = add(y[0], y[2]), sub(y[0], y[2])
    t2, t3 = add(y[1], y[3]), turn(sub(y[1], y[3]), sign)
    return [add(t0, t2), add(t1, t3), sub(t0, t2), sub(t1, t3)]


def dft8(x, sign):
    even = dft4([add(x[k], x[k + 4]) for k in range(4)], sign)
    odd = dft4([scale_root(sub(x[k], x[k + 4]), k, 8, sign) for k in range(4)], sign)
    return [even[0], odd[0], even[1], odd[1], even[2], odd[2], even[3], odd[3]]


def dft16(x, sign):
    first = [dft4([x[4 * a + b] for a in range(4)], sign) for b in range(4)]
    out = [None] * 16
    for c in range(4):
        last = dft4([scale_root(first[b][c], b * c, 16, sign) for b in range(4)], sign)
        for e in range(4):
            out[c + 4 * e] = last[e]
    return out


STR = 1032


def rows_of(i, at):
    start = i * STR + at * 8
    if STR % 8 == 0 and not isinstance(start, int):
        start = pl.multiple_of(start, 8)
    return pl.ds(start, 8)


def get(re_ref, im_ref, i, at):
    rows = rows_of(i, at)
    return (re_ref[rows, :], im_ref[rows, :])


def put(re_ref, im_ref, i, at, x):
    rows = rows_of(i, at)
    re_ref[rows, :] = x[0]
    im_ref[rows, :] = x[1]


def transform_128(re_ref, im_ref, i, sign):
    for b in range(16):
        x = dft8([get(re_ref, im_ref, i, 16 * a + b) for a in range(8)], sign)
        for c in range(8):
            put(re_ref, im_ref, i, 16 * c + b, scale_root(x[c], b * c, 128, sign))
    for c in range(8):
        x = dft16([get(re_ref, im_ref, i, 16 * c + b) for b in range(16)], sign)
        for e in range(16):
            put(re_ref, im_ref, i, 16 * c + e, x[e])


def repeat(count, step, together=1):
    def body(k, carry):
        for u in range(together):
            step(together * k + u)
        return carry

    lax.fori_loop(0, count // together, body, 0)


def place(k):
    return 16 * (k % 8) + k // 8


def encode(blocks, store):
    tops = [jnp.abs(x) for x in blocks]
    while len(tops) > 1:
        tops = [jnp.maximum(x, y) for x, y in zip(tops[::2], tops[1::2])] + tops[len(tops) // 2 * 2 :]
    scale = jnp.maximum(tops[0] * (1.0 / span), 1e-35).astype(bf16)
    inverse = 1.0 / scale.astype(f32)
    for k in range(len(blocks) // 2):
        pair = jnp.concatenate([blocks[2 * k] * inverse, blocks[2 * k + 1] * inverse], axis=0)
        store(slice(16 * k, 16 * k + 16), jnp.exp2(pair).astype(bf16))
    store(slice(8 * len(blocks), 8 * len(blocks) + 8), scale)


def decode_scale(rows):
    return rows.astype(f32) * (1.0 / ln2)


def decode_pair(rows):
    logs = jnp.log(rows.astype(f32))
    return logs[0:8], logs[8:16]


def forward_kernel(x_ref, table_ref, out_ref, re_ref, im_ref):
    def first(pair):
        both = [x_ref[64 * r + pair].astype(f32) for r in range(8)]
        for odd in range(2):
            m = 2 * pair + odd
            x = [v[8 * odd : 8 * odd + 8] for v in both]
            s = [x[k] + x[k + 4] for k in range(4)]
            d = [x[k] - x[k + 4] for k in range(4)]
            s02, s13 = s[0] + s[2], s[1] + s[3]
            put(re_ref, im_ref, 0, m, (s02 + s13, jnp.zeros_like(s02)))
            low, high = (d[1] - d[3]) * half_root, (d[1] + d[3]) * half_root
            rows = [None, (d[0] + low, -d[2] - high), (s[0] - s[2], s[3] - s[1]), (d[0] - low, d[2] - high)]
            for i in range(1, 4):
                put(re_ref, im_ref, i, m, times(rows[i], table_ref[16 * m + i], table_ref[16 * m + 8 + i]))
            mid = s02 - s13
            put(re_ref, im_ref, 4, m, (mid * table_ref[16 * m + 4], mid * table_ref[16 * m + 12]))

    repeat(64, first)

    def second(i):
        transform_128(re_ref, im_ref, i, -1)

    repeat(5, second)

    def third(d):
        blocks = []
        for i in range(5):
            blocks += get(re_ref, im_ref, i, place(d))

        def store(rows, v):
            out_ref[d, rows, :] = v

        encode(blocks, store)

    repeat(128, third, TE)


def lane(x, k):
    return jnp.broadcast_to(x[:, k : k + 1], (8, 128))


def filter_kernel(re_ref, im_ref, out_ref):
    for s in range(3):
        blocks = []
        for u in range(8):
            rows = pl.ds(64 * u + 7 - s, 8, stride=8)
            blocks += [re_ref[rows, :], im_ref[rows, :]]

        def store(rows, v):
            out_ref[0, s, rows, :] = v

        encode(blocks, store)


def prepare_kernel(re_ref, im_ref, code_ref, twist_ref, out_re, out_im, cos_ref, sin_ref, far_re, far_im):
    far_re[...] = jnp.zeros((512, 128), f32)
    far_im[...] = jnp.zeros((512, 128), f32)
    for s in range(3):
        scale = decode_scale(code_ref[0, s, 128:136, :])
        for u in range(8):
            lre, lim = decode_pair(code_ref[0, s, 16 * u : 16 * u + 16, :])
            rows = pl.ds(64 * u + s + 1, 8, stride=8)
            far_re[rows, :] = lre * scale
            far_im[rows, :] = lim * scale
    for t in range(64):
        here, there = slice(8 * t, 8 * t + 8), slice(504 - 8 * t, 512 - 8 * t)
        out_re[here, :] = re_ref[here, :] + far_re[there, :]
        out_im[here, :] = im_ref[here, :] - far_im[there, :]
    for a in range(8):
        tab = twist_ref[a]
        for i in range(5):
            cos_ref[a, i] = lane(tab, i)
            sin_ref[a, i] = lane(tab, 8 + i)


def middle_kernel(x_ref, twist_cos, twist_sin, filter_real, filter_imag, table_ref, out_ref,
                  re_ref, im_ref, re2_ref, im2_ref, tc_ref, ts_ref, fr_ref, fi_ref, sems):
    copies = [
        pltpu.make_async_copy(src, dst, sems.at[k])
        for k, (src, dst) in enumerate(
            [(twist_cos, tc_ref), (twist_sin, ts_ref), (filter_real, fr_ref), (filter_imag, fi_ref)]
        )
    ]
    for c in copies:
        c.start()
    copies[0].wait()
    copies[1].wait()

    def first(src):
        a = 8 * (src % 16) + src // 16
        scale = decode_scale(x_ref[src, 80:88, :])
        for i in range(5):
            x = decode_pair(x_ref[src, 16 * i : 16 * i + 16, :])
            put(re_ref, im_ref, i, a, times(x, scale * tc_ref[a, i], scale * ts_ref[a, i]))

    repeat(128, first, TD)

    def second(i):
        transform_128(re_ref, im_ref, i, -1)

    repeat(5, second)
    copies[2].wait()
    copies[3].wait()

    def third(at):
        b = at // 16 + 8 * (at % 16)
        x = []
        for j in range(8):
            across = pl.ds(at * 8 + j, 8, stride=STR)
            x.append((re_ref[across, :], im_ref[across, :]))
        for j in range(1, 8):
            x[j] = times(x[j], table_ref[16 * b + j], table_ref[16 * b + 8 + j])
        x = dft8(x, -1)
        y = []
        for e in range(8):
            rows = pl.ds(pl.multiple_of(8 * b, 8) + 1024 * e, 8)
            y.append(times(x[e], fr_ref[rows, :], fi_ref[rows, :]))
        y = dft8(y, 1)
        for j in range(8):
            if j:
                y[j] = times_conj(y[j], table_ref[16 * b + j], table_ref[16 * b + 8 + j])
            across = pl.ds(b * 8 + j, 8, stride=STR)
            re2_ref[across, :] = y[j][0]
            im2_ref[across, :] = y[j][1]

    repeat(128, third, TM)

    def fourth(i):
        transform_128(re2_ref, im2_ref, i, 1)

    repeat(5, fourth)

    def fifth(src):
        a = 8 * (src % 16) + src // 16
        blocks = []
        for i in range(5):
            blocks += times_conj(get(re2_ref, im2_ref, i, place(a)), tc_ref[a, i], ts_ref[a, i])

        def store(rows, v):
            out_ref[src, rows, :] = v

        encode(blocks, store)

    repeat(128, fifth, TE)


def backward_kernel(x_ref, table_ref, out_ref, re_ref, im_ref, conv_ref):
    def first(d):
        scale = decode_scale(x_ref[d, 80:88, :])
        for i in range(5):
            lre, lim = decode_pair(x_ref[d, 16 * i : 16 * i + 16, :])
            put(re_ref, im_ref, i, d, (lre * scale, lim * scale))

    repeat(128, first, TD)

    def second(i):
        transform_128(re_ref, im_ref, i, 1)

    repeat(5, second)

    def third(at):
        m = at // 16 + 8 * (at % 16)
        u0 = get(re_ref, im_ref, 0, at)[0]
        z = [times_conj(get(re_ref, im_ref, i, at), table_ref[16 * m + i], table_ref[16 * m + 8 + i]) for i in range(1, 4)]
        re4, im4 = get(re_ref, im_ref, 4, at)
        u4 = re4 * table_ref[16 * m + 4] + im4 * table_ref[16 * m + 12]
        (x1, y1), (x2, y2), (x3, y3) = z
        even, odd = u0 + u4, u0 - u4
        x13, y13 = x1 + x3, y1 - y3
        up, down = even + x2, even - x2
        conv_ref[0, m] = up + x13
        conv_ref[4, m] = up - x13
        conv_ref[2, m] = down - y13
        conv_ref[6, m] = down + y13
        aa, bb = (x1 - x3) * half_root, (y1 + y3) * half_root
        up, down = odd + y2, odd - y2
        diff, both = aa - bb, aa + bb
        conv_ref[1, m] = down + diff
        conv_ref[5, m] = down - diff
        conv_ref[3, m] = up - both
        conv_ref[7, m] = up + both

    repeat(128, third)

    def fourth(step):
        r, g = step // 8, step % 8
        blocks = [conv_ref[r, 16 * g + k] * (1.0 / 1048576.0) for k in range(16)]

        def store(rows, v):
            out_ref[r, g, rows, :] = v

        encode(blocks, store)

    repeat(64, fourth, TE)


def gate_kernel(x_ref, value_ref, gate_ref, skip_ref, out_ref):
    skip = skip_ref[0:1, :]

    def body(k):
        start = pl.multiple_of(16 * k, 16)
        for pair in range(4):
            sides = []
            for r in (2 * pair, 2 * pair + 1):
                scale = decode_scale(x_ref[r, 0, 128:136, :])
                low, high = decode_pair(x_ref[r, 0, pl.ds(start, 16), :])
                sides.append((low * scale, high * scale))
            for odd in range(2):
                conv = jnp.concatenate([sides[0][odd], sides[1][odd]], axis=0)
                rows = slice(16 * pair, 16 * pair + 16)
                v = value_ref[2 * k + odd, rows, :].astype(f32)
                g = gate_ref[2 * k + odd, rows, :].astype(f32)
                out_ref[2 * k + odd, rows, :] = (g * (conv + skip * v)).astype(bf16)

    repeat(8, body)


def roots_table(period):
    m, i = np.arange(128)[:, None], np.arange(8)[None, :]
    angle = -2.0 * np.pi * (m * i % period) / period
    return np.concatenate([np.cos(angle), np.sin(angle)], axis=1).astype(np.float32).reshape(-1)


def twist_table(device):
    shape = (128, 8, 128)
    lanes = lax.broadcasted_iota(jnp.int32, shape, 2)
    q = 8 * lax.broadcasted_iota(jnp.int32, shape, 0) + lax.broadcasted_iota(jnp.int32, shape, 1)
    kp = 8 * device + lanes % 8
    angle = (q * kp % 1048576).astype(f32) * (-2.0 * math.pi / 1048576.0)
    return jnp.where(lanes < 8, jnp.cos(angle), jnp.sin(angle))


twist_tables = twist_table


def vspec():
    return pl.BlockSpec(memory_space=pltpu.VMEM)


def sspec():
    return pl.BlockSpec(memory_space=pltpu.SMEM)


def aspec():
    return pl.BlockSpec(memory_space=pl.ANY)


def small_params():
    return params()


def params(mib=56):
    return pltpu.CompilerParams(vmem_limit_bytes=mib * 1024 * 1024)


def forward(columns, table):
    return pl.pallas_call(
        forward_kernel,
        out_shape=jax.ShapeDtypeStruct((128, 88, 128), bf16),
        in_specs=[vspec(), sspec()],
        out_specs=vspec(),
        scratch_shapes=[pltpu.VMEM((5 * STR, 128), f32)] * 2,
        compiler_params=params(16),
        name="forward_columns",
    )(columns, table)


def filter_codes(filter_real, filter_imag):
    rows = pl.BlockSpec((512, 128), lambda g: (g, 0))
    return pl.pallas_call(
        filter_kernel,
        grid=(16,),
        out_shape=jax.ShapeDtypeStruct((16, 3, 136, 128), bf16),
        in_specs=[rows, rows],
        out_specs=pl.BlockSpec((1, 3, 136, 128), lambda g: (g, 0, 0, 0)),
        compiler_params=small_params(),
        cost_estimate=pl.CostEstimate(flops=8000000, bytes_accessed=10 << 20, transcendentals=1000000),
        name="filter_codes",
    )(filter_real, filter_imag)


def prepare(filter_real, filter_imag, codes, twist):
    rows = pl.BlockSpec((512, 128), lambda g: (g, 0))
    wide = pl.BlockSpec((8, 5, 8, 128), lambda g: (g, 0, 0, 0))
    return pl.pallas_call(
        prepare_kernel,
        grid=(16,),
        out_shape=[jax.ShapeDtypeStruct((8192, 128), f32)] * 2 + [jax.ShapeDtypeStruct((128, 5, 8, 128), f32)] * 2,
        in_specs=[
            rows,
            rows,
            pl.BlockSpec((1, 3, 136, 128), lambda g: (15 - g, 0, 0, 0)),
            pl.BlockSpec((8, 8, 128), lambda g: (g, 0, 0)),
        ],
        out_specs=[rows, rows, wide, wide],
        scratch_shapes=[pltpu.VMEM((512, 128), f32)] * 2,
        compiler_params=small_params(),
        cost_estimate=pl.CostEstimate(flops=80000000000, bytes_accessed=25 << 20, transcendentals=1000000),
        name="prepare",
    )(filter_real, filter_imag, codes, twist)


def middle(arrived, twist_cos, twist_sin, filter_real, filter_imag, table):
    return pl.pallas_call(
        middle_kernel,
        out_shape=jax.ShapeDtypeStruct((128, 88, 128), bf16),
        in_specs=[vspec()] + [aspec()] * 4 + [sspec()],
        out_specs=vspec(),
        scratch_shapes=[pltpu.VMEM((8 * STR, 128), f32)] * 4
        + [pltpu.VMEM((128, 5, 8, 128), f32)] * 2
        + [pltpu.VMEM((8192, 128), f32)] * 2
        + [pltpu.SemaphoreType.DMA((4,))],
        compiler_params=params(44),
        name="filter_rows",
    )(arrived, twist_cos, twist_sin, filter_real, filter_imag, table)


def backward(returned, table):
    return pl.pallas_call(
        backward_kernel,
        out_shape=jax.ShapeDtypeStruct((8, 8, 136, 128), bf16),
        in_specs=[vspec(), sspec()],
        out_specs=vspec(),
        scratch_shapes=[pltpu.VMEM((5 * STR, 128), f32)] * 2 + [pltpu.VMEM((8, 128, 8, 128), f32)],
        compiler_params=params(24),
        name="backward_columns",
    )(returned, table)


def gating(settled, value, gate, skip):
    return pl.pallas_call(
        gate_kernel,
        grid=(8,),
        out_shape=jax.ShapeDtypeStruct((128, 64, 128), bf16),
        in_specs=[
            pl.BlockSpec((8, 1, 136, 128), lambda g: (0, g, 0, 0)),
            pl.BlockSpec((16, 64, 128), lambda g: (g, 0, 0)),
            pl.BlockSpec((16, 64, 128), lambda g: (g, 0, 0)),
            pl.BlockSpec((1, 128), lambda g: (0, 0)),
        ],
        out_specs=pl.BlockSpec((16, 64, 128), lambda g: (g, 0, 0)),
        compiler_params=params(16),
        name="gating",
    )(settled, value, gate, skip.reshape(1, 128))


def convolve(value, gate, filter_real, filter_imag, skip):
    device = lax.axis_index("row") * 16 + lax.axis_index("col")
    everyone = ("row", "col")
    table = jnp.asarray(roots_table(1024))
    filter_real = filter_real.reshape(8192, 128)
    filter_imag = filter_imag.reshape(8192, 128)
    pieces = value.reshape(128, 8, 8, 128)
    codes = filter_codes(filter_real, filter_imag)
    columns = lax.all_to_all(pieces, "row", split_axis=1, concat_axis=0, tiled=True)
    columns, codes = lax.optimization_barrier((columns, codes))
    codes = lax.ppermute(codes, everyone, [(d, 127 - d) for d in range(128)])
    spectrum = forward(columns.reshape(512, 16, 128), table)
    twist = twist_table(device)
    arrived = lax.all_to_all(spectrum, everyone, split_axis=0, concat_axis=0, tiled=True)
    both_real, both_imag, twist_cos, twist_sin = prepare(filter_real, filter_imag, codes, twist)
    leaving = middle(arrived, twist_cos, twist_sin, both_real, both_imag, table)
    returned = lax.all_to_all(leaving, everyone, split_axis=0, concat_axis=0, tiled=True)
    convolved = backward(returned, table)
    settled = lax.all_to_all(convolved, "row", split_axis=0, concat_axis=0, tiled=True)
    return gating(settled, value, gate, skip)


def solution(mesh):
    return jax.shard_map(
        convolve,
        mesh=mesh,
        in_specs=(
            P("row", "col", None),
            P("row", "col", None),
            P(None, ("row", "col"), None),
            P(None, ("row", "col"), None),
            P(),
        ),
        out_specs=P("row", "col", None),
        check_vma=False,
    )
```

time: 265 us -> 230 us (0.87)
  blocking collectives: 127 us -> 75.6 us
  waiting for transfers between devices: 53.1 us -> 65.6 us
  starting transfers between devices: 9.6 us -> 16.1 us
  Pallas kernels: 65.1 us -> 61.9 us
    all_to_all x2 -> x1, blocking collectives: 93.8 us -> 44.5 us  [convolve(): lax.all_to_all(leaving, everyone, split_axis=0, concat_axis=0, tiled=True)]
    ppermute x0 -> x1, waiting for transfers between devices: none -> 45.1 us  [convolve(): codes = lax.ppermute(codes, everyone, [(d, 127 - d) for d in range(128)])]
    all_to_all x1 -> x2, waiting for transfers between devices: 53.1 us -> 20.5 us  [the longest x1 20.5 us: convolve(): lax.all_to_all(pieces, 'row', split_axis=1, concat_axis=0, tiled=True)]
    pallas_call x1, Pallas kernels: 12.7 us -> 7.41 us  [backward(): pl.pallas_call(backward_kernel, out_shape=jax.ShapeDtypeStruct((8, 8, 136...]
    pallas_call x2 -> x4, Pallas kernels: 45 us -> 50.1 us  [the longest x1 16.9 us: middle(): pl.pallas_call(middle_kernel, out_shape=jax.ShapeDtypeStruct((128, 88, 12...]
    broadcast_in_dim x2 -> x0, local copies, waits for them, and re-layouts: 5.14 us -> none  [the longest x1 2.6 us: twist_tables(): jnp.broadcast_to(cosine[..., None], wide)]
    all_to_all x1 -> x2, starting transfers between devices: 9.6 us -> 13.3 us  [the longest x1 7.4 us: convolve(): lax.all_to_all(spectrum, everyone, split_axis=0, concat_axis=0, tiled=True)]
    unnamed x0 -> x12, local copies, waits for them, and re-layouts: none -> 3.5 us
  transfers between devices with their start and end apart: 1 -> 3, of which waited for: 1 -> 2; matrix products, arithmetic and copies ran while one was open for 1% -> 1% of each run, Pallas kernels for 0% -> 15%
where the time goes in v2:
time: 230 us; the launch traced here: 229 us
  blocking collectives  75.6 us (33%)
  waiting for transfers between devices  65.6 us (29%)
  Pallas kernels  61.9 us (27%)
  starting transfers between devices  16.1 us (7%)
  local copies, waits for them, and re-layouts  6.79 us (3%)
  other arithmetic  3.18 us (1%)
    ppermute x1, waiting for transfers between devices, convolve(): codes = lax.ppermute(codes, everyone, [(d, 127 - d) for d in range(128)])  45.1 us
    all_to_all x1, blocking collectives, convolve(): lax.all_to_all(leaving, everyone, split_axis=0, concat_axis=0, tiled=True)  44.5 us
    all_to_all x1, blocking collectives, convolve(): lax.all_to_all(convolved, 'row', split_axis=0, concat_axis=0, tiled=True)  31 us
    all_to_all x1, waiting for transfers between devices, convolve(): lax.all_to_all(pieces, 'row', split_axis=1, concat_axis=0, tiled=True)  20.5 us
    pallas_call x1, Pallas kernels, middle(): pl.pallas_call(middle_kernel, out_shape=jax.ShapeDtypeStruct((128, 88, 12...  16.9 us
    pallas_call x1, Pallas kernels, prepare(): pl.pallas_call(prepare_kernel, grid=(16,), out_shape=[jax.ShapeDtypeStruc...  15.2 us
    pallas_call x1, Pallas kernels, filter_codes(): pl.pallas_call(filter_kernel, grid=(16,), out_shape=jax.ShapeDtypeStruct(...  10.7 us
    pallas_call x1, Pallas kernels, forward(): pl.pallas_call(forward_kernel, out_shape=jax.ShapeDtypeStruct((128, 88, 1...  7.43 us
  transfers between devices with their start and end apart: 3, of which 2 were waited for; matrix products, arithmetic and copies ran while one was open for 1% of the time, Pallas kernels for 15%

profile of v2, /device:TPU:0, one launch (start us, length us, event | category | flops | bytes accessed | tf_op | source)
XLA Modules:
  0.0 229.2 jit_solution(17321716599846544061)
XLA Ops:
  0.0 3.3 %copy.8 = bf16[128,8,8,128]{3,2,0,1:T(8,128)(2,1)} copy(bf16[128,8,8,128]{3,2,1,0:T(8,128)(2,1)} %bitcast.11) | data formatting | bytes 4194304 | tf_op jit(solution)/shard_map/reshape | solution.py:506
  3.3 5.9 %all-to-all-start = ((bf16[128,8,8,128]{3,2,0,1:T(8,128)(2,1)}), bf16[128,8,8,128]{3,2,0,1:T(8,128)(2,1)S(1)}, u32[]{:S(2)}, u32[]{:S(2)}) async-start(bf16[128,8,8,128]{3,2,0,1:T(8,128)(2,1)} %copy.8), calls=%async_computation | async-start | bytes 4194304 | tf_op jit(solution)/shard_map/all_to_all | solution.py:508
  9.2 0.0 copy-start.4
  9.2 10.7 %filter_codes.1 = bf16[16,3,136,128]{3,2,1,0:T(8,128)(2,1)} custom-call(f32[8192,128]{1,0:T(8,128)} %bitcast.13, f32[8192,128]{1,0:T(8,128)} %bitcast.15), custom_call_target="tpu_custom_call" | custom-call | flops 8000000 | bytes 10485760 | tf_op jit(solution)/shard_map/filter_codes/pallas_call | solution.py:423
  19.9 20.5 %all-to-all-done = bf16[128,8,8,128]{3,2,0,1:T(8,128)(2,1)S(1)} async-done(((bf16[128,8,8,128]{3,2,0,1:T(8,128)(2,1)}), bf16[128,8,8,128]{3,2,0,1:T(8,128)(2,1)S(1)}, u32[]{:S(2)}, u32[]{:S(2)}) %all-to-all-start) | async-done | bytes 2097184 | tf_op jit(solution)/shard_map/all_to_all | solution.py:508
  40.4 2.8 %collective-permute-start = (bf16[16,3,136,128]{3,2,1,0:T(8,128)(2,1)}, bf16[16,3,136,128]{3,2,1,0:T(8,128)(2,1)}, u32[]{:S(2)}, u32[]{:S(2)}) collective-permute-start(bf16[16,3,136,128]{3,2,1,0:T(8,128)(2,1)} %filter_codes.1), channel_id=1, source_target_pairs={{0,127},{1,126},{2,125},{3,124},{4,123},{5,122},{6,121},{7,120},{8... | collective-permute-start | bytes 5013512 | tf_op jit(solution)/shard_map/ppermute | solution.py:510
  43.2 3.2 %sine_select_fusion.twist_ref = f32[128,8,128]{2,1,0:T(8,128)} fusion(s32[128]{0:T(128)S(1)} %get-tuple-element.19, s32[128]{0:T(128)S(1)} %broadcast_add_fusion, s32[]{:T(128)S(6)} %mul.21, s32[128]{0:T(128)S(1)} %get-tuple-element.20, pred[128]{0:T(512)(128)(4,1)S(1)} %get-tuple-element.17, pred[128]{0:T(512)(128)(4,1)S(1)} %get-tuple-element.18), kind=kLoop, calls=%fused_computation.6 | loop fusion | flops 2359296 | bytes 526084 | tf_op jit(solution)/shard_map/jit(_where)/select_n | solution.py:383
  46.4 0.0 copy-done.4
  46.4 7.4 %forward_columns.1 = bf16[128,88,128]{2,1,0:T(8,128)(2,1)} custom-call(bf16[512,16,128]{2,1,0:T(8,128)(2,1)S(1)} %bitcast.10, f32[2048]{0:T(1024)S(1)} %copy-done.4), custom_call_target="tpu_custom_call" | custom-call | tf_op jit(solution)/shard_map/forward_columns/pallas_call | solution.py:410
  53.8 7.4 %all-to-all-start.1 = ((bf16[128,88,128]{2,1,0:T(8,128)(2,1)}), bf16[128,88,128]{2,1,0:T(8,128)(2,1)}, u32[]{:S(2)}, u32[]{:S(2)}) async-start(bf16[128,88,128]{2,1,0:T(8,128)(2,1)} %forward_columns.1), calls=%async_computation.1 | async-start | bytes 5767168 | tf_op jit(solution)/shard_map/all_to_all | solution.py:513
  61.2 45.1 %collective-permute-done.code_ref = bf16[16,3,136,128]{3,2,1,0:T(8,128)(2,1)} collective-permute-done((bf16[16,3,136,128]{3,2,1,0:T(8,128)(2,1)}, bf16[16,3,136,128]{3,2,1,0:T(8,128)(2,1)}, u32[]{:S(2)}, u32[]{:S(2)}) %collective-permute-start) | collective-permute-done | bytes 1671200 | tf_op jit(solution)/shard_map/ppermute | solution.py:510
  106.3 15.2 %prepare.1 = (f32[8192,128]{1,0:T(8,128)}, f32[8192,128]{1,0:T(8,128)}, f32[128,5,8,128]{3,2,1,0:T(8,128)}, f32[128,5,8,128]{3,2,1,0:T(8,128)}) custom-call(f32[8192,128]{1,0:T(8,128)} %bitcast.14, f32[8192,128]{1,0:T(8,128)} %bitcast.16, bf16[16,3,136,128]{3,2,1,0:T(8,128)(2,1)} %collective-permute-done.code_ref, f32[128,8,128]{2,1,0:T(8,128)} %sine_select_fusion.twist_ref), custom_call_target="tpu_custom_call" | custom-call | flops 80000000000 | bytes 26214400 | tf_op jit(solution)/shard_map/prepare/pallas_call | solution.py:438
  121.5 0.0 all-to-all-done.1.x_ref
  121.5 0.0 copy-start.1
  121.5 1.7 copy-done.1
  123.2 0.0 copy-start.2
  123.2 1.7 copy-done.2
  125.0 16.9 %filter_rows.1 = bf16[128,88,128]{2,1,0:T(8,128)(2,1)S(1)} custom-call(bf16[128,88,128]{2,1,0:T(8,128)(2,1)} %all-to-all-done.1.x_ref, f32[128,5,8,128]{3,2,1,0:T(8,128)S(1)} %copy-done.1, f32[128,5,8,128]{3,2,1,0:T(8,128)S(1)} %copy-done.2, f32[8192,128]{1,0:T(8,128)} %get-tuple-element.15.filter_real, f32[8192,128]{1,0:T(8,128)} %get-tuple-element.16.filter_imag, ...), custom_call_target="tpu_custom_call" | custom-call | tf_op jit(solution)/shard_map/filter_rows/pallas_call | solution.py:457
  141.9 44.5 %all_to_all.33.x_ref = bf16[128,88,128]{2,1,0:T(8,128)(2,1)S(1)} all-to-all(bf16[128,88,128]{2,1,0:T(8,128)(2,1)S(1)} %filter_rows.1), channel_id=1, replica_groups=mesh['row'=8,'col'=16] {'row','col'}, dimensions={0} | all-to-all | bytes 5767168 | tf_op jit(solution)/shard_map/all_to_all | solution.py:516
  186.4 7.4 %backward_columns.1 = bf16[8,8,136,128]{3,2,1,0:T(8,128)(2,1)S(1)} custom-call(bf16[128,88,128]{2,1,0:T(8,128)(2,1)S(1)} %all_to_all.33.x_ref, f32[2048]{0:T(1024)S(1)} %copy-done.4), custom_call_target="tpu_custom_call" | custom-call | tf_op jit(solution)/shard_map/backward_columns/pallas_call | solution.py:472
  193.8 0.0 copy-start
  193.8 0.0 copy-start.3
  193.8 0.0 copy-start.5
  193.8 31.0 %all_to_all.34.x_ref = bf16[8,8,136,128]{3,2,1,0:T(8,128)(2,1)S(1)} all-to-all(bf16[8,8,136,128]{3,2,1,0:T(8,128)(2,1)S(1)} %backward_columns.1), channel_id=1, replica_groups=mesh['row'=8,'col'=16] {'row'}, dimensions={0} | all-to-all | bytes 4456448 | tf_op jit(solution)/shard_map/all_to_all | solution.py:518
  224.9 0.0 copy-done
  224.9 0.0 copy-done.3
  224.9 0.0 copy-done.5
  224.9 4.3 %gating.1 = bf16[128,64,128]{2,1,0:T(8,128)(2,1)} custom-call(bf16[8,8,136,128]{3,2,1,0:T(8,128)(2,1)S(1)} %all_to_all.34.x_ref, bf16[128,64,128]{2,1,0:T(8,128)(2,1)S(1)} %copy-done, bf16[128,64,128]{2,1,0:T(8,128)(2,1)S(1)} %copy-done.3, f32[1,128]{1,0:T(1,128)S(1)} %bitcast.12), custom_call_target="tpu_custom_call" | custom-call | tf_op jit(solution)/shard_map/gating/pallas_call | solution.py:484
  (3 shorter events, 0.0 us)
Async XLA Ops:
  3.3 37.1 %all-to-all-start = ((bf16[128,8,8,128]{3,2,0,1:T(8,128)(2,1)}), bf16[128,8,8,128]{3,2,0,1:T(8,128)(2,1)S(1)}, u32[]{:S(2)}, u32[]{:S(2)}) async-start(bf16[128,8,8,128]{3,2,0,1:T(8,128)(2,1)} %copy.8), calls=%async_computation | async-start | bytes 4194304 | tf_op jit(solution)/shard_map/all_to_all | solution.py:508
  9.2 37.2 %copy-start.4 = (f32[2048]{0:T(1024)S(1)}, f32[2048]{0:T(1024)}, u32[]{:S(2)}) copy-start(f32[2048]{0:T(1024)} %constant.43.clone.table_ref) | copy-start | bytes 24580
  40.4 66.0 %collective-permute-start = (bf16[16,3,136,128]{3,2,1,0:T(8,128)(2,1)}, bf16[16,3,136,128]{3,2,1,0:T(8,128)(2,1)}, u32[]{:S(2)}, u32[]{:S(2)}) collective-permute-start(bf16[16,3,136,128]{3,2,1,0:T(8,128)(2,1)} %filter_codes.1), channel_id=1, source_target_pairs={{0,127},{1,126},{2,125},{3,124},{4,123},{5,122},{6,121},{7,120},{8... | collective-permute-start | bytes 5013512 | tf_op jit(solution)/shard_map/ppermute | solution.py:510
  53.8 67.7 %all-to-all-start.1 = ((bf16[128,88,128]{2,1,0:T(8,128)(2,1)}), bf16[128,88,128]{2,1,0:T(8,128)(2,1)}, u32[]{:S(2)}, u32[]{:S(2)}) async-start(bf16[128,88,128]{2,1,0:T(8,128)(2,1)} %forward_columns.1), calls=%async_computation.1 | async-start | bytes 5767168 | tf_op jit(solution)/shard_map/all_to_all | solution.py:513
  121.5 1.7 copy-start.1
  123.2 1.7 copy-start.2
  193.8 31.1 %copy-start = (bf16[128,64,128]{2,1,0:T(8,128)(2,1)S(1)}, bf16[128,64,128]{2,1,0:T(8,128)(2,1)}, u32[]{:S(2)}) copy-start(bf16[128,64,128]{2,1,0:T(8,128)(2,1)} %value_ref.1) | copy-start | bytes 6291460
  193.8 31.1 %copy-start.3 = (bf16[128,64,128]{2,1,0:T(8,128)(2,1)S(1)}, bf16[128,64,128]{2,1,0:T(8,128)(2,1)}, u32[]{:S(2)}) copy-start(bf16[128,64,128]{2,1,0:T(8,128)(2,1)} %gate_ref.1) | copy-start | bytes 6291460
  193.8 31.1 %copy-start.5 = (f32[128]{0:T(128)S(1)}, f32[128]{0:T(128)}, u32[]{:S(2)}) copy-start(f32[128]{0:T(128)} %param.10) | copy-start | bytes 1540

commit v3 on v2

--- a/solution.py
+++ b/solution.py
@@ -8,9 +8,11 @@
 from jax.experimental.pallas import tpu as pltpu
 from jax.sharding import PartitionSpec as P
 
-TM = 4
-TE = 8
-TD = 8
+GS = 2
+TG = 4
+TM = 1
+TE = 16
+TD = 16
 half_root = math.sqrt(0.5)
 span = 124.0
 ln2 = math.log(2.0)
@@ -85,7 +87,7 @@
     return out
 
 
-STR = 1032
+STR = 1096
 
 
 def rows_of(i, at):
@@ -108,13 +110,13 @@
 
 def transform_128(re_ref, im_ref, i, sign):
     for b in range(16):
-        x = dft8([get(re_ref, im_ref, i, 16 * a + b) for a in range(8)], sign)
+        x = dft8([get(re_ref, im_ref, i, 17 * a + b) for a in range(8)], sign)
         for c in range(8):
-            put(re_ref, im_ref, i, 16 * c + b, scale_root(x[c], b * c, 128, sign))
+            put(re_ref, im_ref, i, 17 * c + b, scale_root(x[c], b * c, 128, sign))
     for c in range(8):
-        x = dft16([get(re_ref, im_ref, i, 16 * c + b) for b in range(16)], sign)
+        x = dft16([get(re_ref, im_ref, i, 17 * c + b) for b in range(16)], sign)
         for e in range(16):
-            put(re_ref, im_ref, i, 16 * c + e, x[e])
+            put(re_ref, im_ref, i, 17 * c + e, x[e])
 
 
 def repeat(count, step, together=1):
@@ -126,8 +128,12 @@
     lax.fori_loop(0, count // together, body, 0)
 
 
+def slot(n):
+    return 17 * (n // 16) + n % 16
+
+
 def place(k):
-    return 16 * (k % 8) + k // 8
+    return 17 * (k % 8) + k // 8
 
 
 def encode(blocks, store):
@@ -156,17 +162,18 @@
         both = [x_ref[64 * r + pair].astype(f32) for r in range(8)]
         for odd in range(2):
             m = 2 * pair + odd
+            at = slot(m)
             x = [v[8 * odd : 8 * odd + 8] for v in both]
             s = [x[k] + x[k + 4] for k in range(4)]
             d = [x[k] - x[k + 4] for k in range(4)]
             s02, s13 = s[0] + s[2], s[1] + s[3]
-            put(re_ref, im_ref, 0, m, (s02 + s13, jnp.zeros_like(s02)))
+            put(re_ref, im_ref, 0, at, (s02 + s13, jnp.zeros_like(s02)))
             low, high = (d[1] - d[3]) * half_root, (d[1] + d[3]) * half_root
             rows = [None, (d[0] + low, -d[2] - high), (s[0] - s[2], s[3] - s[1]), (d[0] - low, d[2] - high)]
             for i in range(1, 4):
-                put(re_ref, im_ref, i, m, times(rows[i], table_ref[16 * m + i], table_ref[16 * m + 8 + i]))
+                put(re_ref, im_ref, i, at, times(rows[i], table_ref[16 * m + i], table_ref[16 * m + 8 + i]))
             mid = s02 - s13
-            put(re_ref, im_ref, 4, m, (mid * table_ref[16 * m + 4], mid * table_ref[16 * m + 12]))
+            put(re_ref, im_ref, 4, at, (mid * table_ref[16 * m + 4], mid * table_ref[16 * m + 12]))
 
     repeat(64, first)
 
@@ -205,78 +212,94 @@
         encode(blocks, store)
 
 
-def prepare_kernel(re_ref, im_ref, code_ref, twist_ref, out_re, out_im, cos_ref, sin_ref, far_re, far_im):
-    far_re[...] = jnp.zeros((512, 128), f32)
-    far_im[...] = jnp.zeros((512, 128), f32)
-    for s in range(3):
-        scale = decode_scale(code_ref[0, s, 128:136, :])
-        for u in range(8):
-            lre, lim = decode_pair(code_ref[0, s, 16 * u : 16 * u + 16, :])
-            rows = pl.ds(64 * u + s + 1, 8, stride=8)
-            far_re[rows, :] = lre * scale
-            far_im[rows, :] = lim * scale
-    for t in range(64):
-        here, there = slice(8 * t, 8 * t + 8), slice(504 - 8 * t, 512 - 8 * t)
-        out_re[here, :] = re_ref[here, :] + far_re[there, :]
-        out_im[here, :] = im_ref[here, :] - far_im[there, :]
-    for a in range(8):
+def twist_kernel(twist_ref, cos_ref, sin_ref):
+    for a in range(32):
         tab = twist_ref[a]
         for i in range(5):
             cos_ref[a, i] = lane(tab, i)
             sin_ref[a, i] = lane(tab, 8 + i)
 
 
-def middle_kernel(x_ref, twist_cos, twist_sin, filter_real, filter_imag, table_ref, out_ref,
+def merge_kernel(re_ref, im_ref, code_ref, out_re, out_im, far_re, far_im):
+    far_re[...] = jnp.zeros((1024, 128), f32)
+    far_im[...] = jnp.zeros((1024, 128), f32)
+    for g in range(2):
+        for s in range(3):
+            scale = decode_scale(code_ref[g, s, 128:136, :])
+            for u in range(8):
+                lre, lim = decode_pair(code_ref[g, s, 16 * u : 16 * u + 16, :])
+                rows = pl.ds(512 * g + 64 * u + s + 1, 8, stride=8)
+                far_re[rows, :] = lre * scale
+                far_im[rows, :] = lim * scale
+    for t in range(128):
+        here, there = slice(8 * t, 8 * t + 8), slice(1016 - 8 * t, 1024 - 8 * t)
+        out_re[here, :] = re_ref[here, :] + far_re[there, :]
+        out_im[here, :] = im_ref[here, :] - far_im[there, :]
+
+
+def middle_kernel(x_ref, twist_cos, twist_sin, filter_real, filter_imag, root_ref, out_ref,
                   re_ref, im_ref, re2_ref, im2_ref, tc_ref, ts_ref, fr_ref, fi_ref, sems):
-    copies = [
-        pltpu.make_async_copy(src, dst, sems.at[k])
-        for k, (src, dst) in enumerate(
-            [(twist_cos, tc_ref), (twist_sin, ts_ref), (filter_real, fr_ref), (filter_imag, fi_ref)]
+    parts = []
+    for k in range(4):
+        rows = pl.ds(32 * k, 32)
+        parts.append(
+            [
+                pltpu.make_async_copy(twist_cos.at[rows], tc_ref.at[rows], sems.at[2 * k]),
+                pltpu.make_async_copy(twist_sin.at[rows], ts_ref.at[rows], sems.at[2 * k + 1]),
+            ]
         )
-    ]
-    for c in copies:
-        c.start()
-    copies[0].wait()
-    copies[1].wait()
+    parts.append(
+        [
+            pltpu.make_async_copy(filter_real, fr_ref, sems.at[8]),
+            pltpu.make_async_copy(filter_imag, fi_ref, sems.at[9]),
+        ]
+    )
+    for part in parts:
+        for c in part:
+            c.start()
 
     def first(src):
         a = 8 * (src % 16) + src // 16
         scale = decode_scale(x_ref[src, 80:88, :])
         for i in range(5):
             x = decode_pair(x_ref[src, 16 * i : 16 * i + 16, :])
-            put(re_ref, im_ref, i, a, times(x, scale * tc_ref[a, i], scale * ts_ref[a, i]))
-
-    repeat(128, first, TD)
+            put(re_ref, im_ref, i, slot(a), times(x, scale * tc_ref[src, i], scale * ts_ref[src, i]))
+
+    for k in range(4):
+        for c in parts[k]:
+            c.wait()
+        repeat(32, lambda src, k=k: first(32 * k + src), TD)
 
     def second(i):
         transform_128(re_ref, im_ref, i, -1)
 
     repeat(5, second)
-    copies[2].wait()
-    copies[3].wait()
-
-    def third(at):
-        b = at // 16 + 8 * (at % 16)
-        x = []
-        for j in range(8):
-            across = pl.ds(at * 8 + j, 8, stride=STR)
-            x.append((re_ref[across, :], im_ref[across, :]))
-        for j in range(1, 8):
-            x[j] = times(x[j], table_ref[16 * b + j], table_ref[16 * b + 8 + j])
-        x = dft8(x, -1)
-        y = []
-        for e in range(8):
-            rows = pl.ds(pl.multiple_of(8 * b, 8) + 1024 * e, 8)
-            y.append(times(x[e], fr_ref[rows, :], fi_ref[rows, :]))
-        y = dft8(y, 1)
-        for j in range(8):
-            if j:
-                y[j] = times_conj(y[j], table_ref[16 * b + j], table_ref[16 * b + 8 + j])
-            across = pl.ds(b * 8 + j, 8, stride=STR)
-            re2_ref[across, :] = y[j][0]
-            im2_ref[across, :] = y[j][1]
-
-    repeat(128, third, TM)
+    for c in parts[4]:
+        c.wait()
+
+    def third(e):
+        start = 136 * (e // 2) + 64 * (e % 2)
+        for i in range(5):
+            x = []
+            for j in range(8):
+                rows = pl.ds(i * STR + 8 * e + j, 8, stride=136)
+                x.append((re_ref[rows, :], im_ref[rows, :]))
+            for j in range(1, 8):
+                x[j] = times(x[j], root_ref[0, e, j], root_ref[1, e, j])
+            x = dft8(x, -1)
+            y = []
+            for k in range(8):
+                rows = pl.ds(64 * e + 1024 * k + i, 8, stride=8)
+                y.append(times(x[k], fr_ref[rows, :], fi_ref[rows, :]))
+            y = dft8(y, 1)
+            for j in range(8):
+                if j:
+                    y[j] = times_conj(y[j], root_ref[0, e, j], root_ref[1, e, j])
+                rows = pl.ds(i * STR + start + j, 8, stride=8)
+                re2_ref[rows, :] = y[j][0]
+                im2_ref[rows, :] = y[j][1]
+
+    repeat(16, third, TM)
 
     def fourth(i):
         transform_128(re2_ref, im2_ref, i, 1)
@@ -287,7 +310,7 @@
         a = 8 * (src % 16) + src // 16
         blocks = []
         for i in range(5):
-            blocks += times_conj(get(re2_ref, im2_ref, i, place(a)), tc_ref[a, i], ts_ref[a, i])
+            blocks += times_conj(get(re2_ref, im2_ref, i, place(a)), tc_ref[src, i], ts_ref[src, i])
 
         def store(rows, v):
             out_ref[src, rows, :] = v
@@ -302,7 +325,7 @@
         scale = decode_scale(x_ref[d, 80:88, :])
         for i in range(5):
             lre, lim = decode_pair(x_ref[d, 16 * i : 16 * i + 16, :])
-            put(re_ref, im_ref, i, d, (lre * scale, lim * scale))
+            put(re_ref, im_ref, i, slot(d), (lre * scale, lim * scale))
 
     repeat(128, first, TD)
 
@@ -311,8 +334,8 @@
 
     repeat(5, second)
 
-    def third(at):
-        m = at // 16 + 8 * (at % 16)
+    def third(m):
+        at = place(m)
         u0 = get(re_ref, im_ref, 0, at)[0]
         z = [times_conj(get(re_ref, im_ref, i, at), table_ref[16 * m + i], table_ref[16 * m + 8 + i]) for i in range(1, 4)]
         re4, im4 = get(re_ref, im_ref, 4, at)
@@ -350,22 +373,23 @@
 def gate_kernel(x_ref, value_ref, gate_ref, skip_ref, out_ref):
     skip = skip_ref[0:1, :]
 
-    def body(k):
+    def body(at):
+        g, k = at // 8, at % 8
         start = pl.multiple_of(16 * k, 16)
         for pair in range(4):
             sides = []
             for r in (2 * pair, 2 * pair + 1):
-                scale = decode_scale(x_ref[r, 0, 128:136, :])
-                low, high = decode_pair(x_ref[r, 0, pl.ds(start, 16), :])
+                scale = decode_scale(x_ref[r, g, 128:136, :])
+                low, high = decode_pair(x_ref[r, g, pl.ds(start, 16), :])
                 sides.append((low * scale, high * scale))
             for odd in range(2):
                 conv = jnp.concatenate([sides[0][odd], sides[1][odd]], axis=0)
                 rows = slice(16 * pair, 16 * pair + 16)
-                v = value_ref[2 * k + odd, rows, :].astype(f32)
-                g = gate_ref[2 * k + odd, rows, :].astype(f32)
-                out_ref[2 * k + odd, rows, :] = (g * (conv + skip * v)).astype(bf16)
-
-    repeat(8, body)
+                v = value_ref[2 * at + odd, rows, :].astype(f32)
+                w = gate_ref[2 * at + odd, rows, :].astype(f32)
+                out_ref[2 * at + odd, rows, :] = (w * (conv + skip * v)).astype(bf16)
+
+    repeat(64 // GS, body, TG)
 
 
 def roots_table(period):
@@ -374,10 +398,18 @@
     return np.concatenate([np.cos(angle), np.sin(angle)], axis=1).astype(np.float32).reshape(-1)
 
 
+def wide_roots():
+    e, j, c = np.arange(16)[:, None, None], np.arange(8)[None, :, None], np.arange(8)[None, None, :]
+    angle = -2.0 * np.pi * (j * (c + 8 * e) % 1024) / 1024
+    both = np.stack([np.cos(angle), np.sin(angle)]).astype(np.float32)
+    return np.broadcast_to(both[..., None], (2, 16, 8, 8, 128))
+
+
 def twist_table(device):
     shape = (128, 8, 128)
     lanes = lax.broadcasted_iota(jnp.int32, shape, 2)
-    q = 8 * lax.broadcasted_iota(jnp.int32, shape, 0) + lax.broadcasted_iota(jnp.int32, shape, 1)
+    source = lax.broadcasted_iota(jnp.int32, shape, 0)
+    q = 64 * (source % 16) + 8 * (source // 16) + lax.broadcasted_iota(jnp.int32, shape, 1)
     kp = 8 * device + lanes % 8
     angle = (q * kp % 1048576).astype(f32) * (-2.0 * math.pi / 1048576.0)
     return jnp.where(lanes < 8, jnp.cos(angle), jnp.sin(angle))
@@ -432,38 +464,46 @@
     )(filter_real, filter_imag)
 
 
-def prepare(filter_real, filter_imag, codes, twist):
-    rows = pl.BlockSpec((512, 128), lambda g: (g, 0))
-    wide = pl.BlockSpec((8, 5, 8, 128), lambda g: (g, 0, 0, 0))
-    return pl.pallas_call(
-        prepare_kernel,
-        grid=(16,),
-        out_shape=[jax.ShapeDtypeStruct((8192, 128), f32)] * 2 + [jax.ShapeDtypeStruct((128, 5, 8, 128), f32)] * 2,
-        in_specs=[
-            rows,
-            rows,
-            pl.BlockSpec((1, 3, 136, 128), lambda g: (15 - g, 0, 0, 0)),
-            pl.BlockSpec((8, 8, 128), lambda g: (g, 0, 0)),
-        ],
-        out_specs=[rows, rows, wide, wide],
-        scratch_shapes=[pltpu.VMEM((512, 128), f32)] * 2,
+def twists(twist):
+    wide = pl.BlockSpec((32, 5, 8, 128), lambda g: (g, 0, 0, 0))
+    return pl.pallas_call(
+        twist_kernel,
+        grid=(4,),
+        out_shape=[jax.ShapeDtypeStruct((128, 5, 8, 128), f32)] * 2,
+        in_specs=[pl.BlockSpec((32, 8, 128), lambda g: (g, 0, 0))],
+        out_specs=[wide, wide],
         compiler_params=small_params(),
-        cost_estimate=pl.CostEstimate(flops=80000000000, bytes_accessed=25 << 20, transcendentals=1000000),
-        name="prepare",
-    )(filter_real, filter_imag, codes, twist)
+        cost_estimate=pl.CostEstimate(flops=8000000, bytes_accessed=6 << 20, transcendentals=0),
+        name="twists",
+    )(twist)
+
+
+def merged(filter_real, filter_imag, codes):
+    rows = pl.BlockSpec((1024, 128), lambda g: (g, 0))
+    return pl.pallas_call(
+        merge_kernel,
+        grid=(8,),
+        out_shape=[jax.ShapeDtypeStruct((8192, 128), f32)] * 2,
+        in_specs=[rows, rows, pl.BlockSpec((2, 3, 136, 128), lambda g: (7 - g, 0, 0, 0))],
+        out_specs=[rows, rows],
+        scratch_shapes=[pltpu.VMEM((1024, 128), f32)] * 2,
+        compiler_params=small_params(),
+        cost_estimate=pl.CostEstimate(flops=80000000000, bytes_accessed=18 << 20, transcendentals=0),
+        name="merge_filters",
+    )(filter_real, filter_imag, codes)
 
 
 def middle(arrived, twist_cos, twist_sin, filter_real, filter_imag, table):
     return pl.pallas_call(
         middle_kernel,
         out_shape=jax.ShapeDtypeStruct((128, 88, 128), bf16),
-        in_specs=[vspec()] + [aspec()] * 4 + [sspec()],
+        in_specs=[vspec()] + [aspec()] * 4 + [vspec()],
         out_specs=vspec(),
         scratch_shapes=[pltpu.VMEM((8 * STR, 128), f32)] * 4
         + [pltpu.VMEM((128, 5, 8, 128), f32)] * 2
         + [pltpu.VMEM((8192, 128), f32)] * 2
-        + [pltpu.SemaphoreType.DMA((4,))],
-        compiler_params=params(44),
+        + [pltpu.SemaphoreType.DMA((10,))],
+        compiler_params=params(50),
         name="filter_rows",
     )(arrived, twist_cos, twist_sin, filter_real, filter_imag, table)
 
@@ -483,15 +523,15 @@
 def gating(settled, value, gate, skip):
     return pl.pallas_call(
         gate_kernel,
-        grid=(8,),
+        grid=(GS,),
         out_shape=jax.ShapeDtypeStruct((128, 64, 128), bf16),
         in_specs=[
-            pl.BlockSpec((8, 1, 136, 128), lambda g: (0, g, 0, 0)),
-            pl.BlockSpec((16, 64, 128), lambda g: (g, 0, 0)),
-            pl.BlockSpec((16, 64, 128), lambda g: (g, 0, 0)),
+            pl.BlockSpec((8, 8 // GS, 136, 128), lambda g: (0, g, 0, 0)),
+            pl.BlockSpec((128 // GS, 64, 128), lambda g: (g, 0, 0)),
+            pl.BlockSpec((128 // GS, 64, 128), lambda g: (g, 0, 0)),
             pl.BlockSpec((1, 128), lambda g: (0, 0)),
         ],
-        out_specs=pl.BlockSpec((16, 64, 128), lambda g: (g, 0, 0)),
+        out_specs=pl.BlockSpec((128 // GS, 64, 128), lambda g: (g, 0, 0)),
         compiler_params=params(16),
         name="gating",
     )(settled, value, gate, skip.reshape(1, 128))
@@ -509,10 +549,12 @@
     columns, codes = lax.optimization_barrier((columns, codes))
     codes = lax.ppermute(codes, everyone, [(d, 127 - d) for d in range(128)])
     spectrum = forward(columns.reshape(512, 16, 128), table)
+    spectrum, device = lax.optimization_barrier((spectrum, device))
     twist = twist_table(device)
     arrived = lax.all_to_all(spectrum, everyone, split_axis=0, concat_axis=0, tiled=True)
-    both_real, both_imag, twist_cos, twist_sin = prepare(filter_real, filter_imag, codes, twist)
-    leaving = middle(arrived, twist_cos, twist_sin, both_real, both_imag, table)
+    twist_cos, twist_sin = twists(twist)
+    both_real, both_imag = merged(filter_real, filter_imag, codes)
+    leaving = middle(arrived, twist_cos, twist_sin, both_real, both_imag, jnp.asarray(wide_roots()))
     returned = lax.all_to_all(leaving, everyone, split_axis=0, concat_axis=0, tiled=True)
     convolved = backward(returned, table)
     settled = lax.all_to_all(convolved, "row", split_axis=0, concat_axis=0, tiled=True)

time: 230 us -> 225 us (0.978)
  waiting for transfers between devices: 65.6 us -> 61.2 us
  blocking collectives: 75.6 us -> 78.9 us
  local copies, waits for them, and re-layouts: 6.79 us -> 3.65 us
    ppermute x1, waiting for transfers between devices: 45.1 us -> 38.9 us  [convolve(): codes = lax.ppermute(codes, everyone, [(d, 127 - d) for d in range(128)])]
    unnamed x12, local copies, waits for them, and re-layouts: 3.5 us -> 0.03 us
    all_to_all x1, blocking collectives: 44.5 us -> 47.8 us  [convolve(): lax.all_to_all(leaving, everyone, split_axis=0, concat_axis=0, tiled=True)]
    pallas_call x2 -> x3, Pallas kernels: 19.5 us -> 18 us  [the longest x1 10 us: merged(): pl.pallas_call(merge_kernel, grid=(8,), out_shape=[jax.ShapeDtypeStruct((...]
  transfers between devices with their start and end apart: 3 -> 3, of which waited for: 2 -> 3; matrix products, arithmetic and copies ran while one was open for 1% -> 2% of each run, Pallas kernels for 15% -> 15%
where the time goes in v3:
time: 225 us; the launch traced here: 224 us
  blocking collectives  78.9 us (35%)
  waiting for transfers between devices  61.2 us (27%)
  Pallas kernels  60.3 us (27%)
  starting transfers between devices  16.1 us (7%)
  local copies, waits for them, and re-layouts  3.65 us (2%)
  other arithmetic  3.53 us (2%)
    all_to_all x1, blocking collectives, convolve(): lax.all_to_all(leaving, everyone, split_axis=0, concat_axis=0, tiled=True)  47.8 us
    ppermute x1, waiting for transfers between devices, convolve(): codes = lax.ppermute(codes, everyone, [(d, 127 - d) for d in range(128)])  38.9 us
    all_to_all x1, blocking collectives, convolve(): lax.all_to_all(convolved, 'row', split_axis=0, concat_axis=0, tiled=True)  31 us
    all_to_all x1, waiting for transfers between devices, convolve(): lax.all_to_all(pieces, 'row', split_axis=1, concat_axis=0, tiled=True)  20.5 us
    pallas_call x1, Pallas kernels, middle(): pl.pallas_call(middle_kernel, out_shape=jax.ShapeDtypeStruct((128, 88, 12...  16.4 us
    pallas_call x1, Pallas kernels, filter_codes(): pl.pallas_call(filter_kernel, grid=(16,), out_shape=jax.ShapeDtypeStruct(...  10.7 us
    pallas_call x1, Pallas kernels, merged(): pl.pallas_call(merge_kernel, grid=(8,), out_shape=[jax.ShapeDtypeStruct((...  10 us
    pallas_call x1, Pallas kernels, forward(): pl.pallas_call(forward_kernel, out_shape=jax.ShapeDtypeStruct((128, 88, 1...  7.62 us
  transfers between devices with their start and end apart: 3, of which 3 were waited for; matrix products, arithmetic and copies ran while one was open for 2% of the time, Pallas kernels for 15%

profile of v3, /device:TPU:0, one launch (start us, length us, event | category | flops | bytes accessed | tf_op | source)
XLA Modules:
  0.0 223.7 jit_solution(17458495474611031245)
XLA Ops:
  0.0 3.3 %copy.9 = bf16[128,8,8,128]{3,2,0,1:T(8,128)(2,1)} copy(bf16[128,8,8,128]{3,2,1,0:T(8,128)(2,1)} %bitcast.11) | data formatting | bytes 4194304 | tf_op jit(solution)/shard_map/reshape | solution.py:546
  3.3 5.9 %all-to-all-start = ((bf16[128,8,8,128]{3,2,0,1:T(8,128)(2,1)}), bf16[128,8,8,128]{3,2,0,1:T(8,128)(2,1)S(1)}, u32[]{:S(2)}, u32[]{:S(2)}) async-start(bf16[128,8,8,128]{3,2,0,1:T(8,128)(2,1)} %copy.9), calls=%async_computation | async-start | bytes 4194304 | tf_op jit(solution)/shard_map/all_to_all | solution.py:548
  9.2 0.0 copy-start.3
  9.2 10.7 %filter_codes.1 = bf16[16,3,136,128]{3,2,1,0:T(8,128)(2,1)} custom-call(f32[8192,128]{1,0:T(8,128)} %bitcast.13, f32[8192,128]{1,0:T(8,128)} %bitcast.15), custom_call_target="tpu_custom_call" | custom-call | flops 8000000 | bytes 10485760 | tf_op jit(solution)/shard_map/filter_codes/pallas_call | solution.py:455
  19.9 20.5 %all-to-all-done = bf16[128,8,8,128]{3,2,0,1:T(8,128)(2,1)S(1)} async-done(((bf16[128,8,8,128]{3,2,0,1:T(8,128)(2,1)}), bf16[128,8,8,128]{3,2,0,1:T(8,128)(2,1)S(1)}, u32[]{:S(2)}, u32[]{:S(2)}) %all-to-all-start) | async-done | bytes 2097184 | tf_op jit(solution)/shard_map/all_to_all | solution.py:548
  40.4 2.8 %collective-permute-start = (bf16[16,3,136,128]{3,2,1,0:T(8,128)(2,1)}, bf16[16,3,136,128]{3,2,1,0:T(8,128)(2,1)}, u32[]{:S(2)}, u32[]{:S(2)}) collective-permute-start(bf16[16,3,136,128]{3,2,1,0:T(8,128)(2,1)} %filter_codes.1), channel_id=1, source_target_pairs={{0,127},{1,126},{2,125},{3,124},{4,123},{5,122},{6,121},{7,120},{8... | collective-permute-start | bytes 5013512 | tf_op jit(solution)/shard_map/ppermute | solution.py:550
  43.2 0.0 copy-done.3
  43.2 7.6 %forward_columns.1 = bf16[128,88,128]{2,1,0:T(8,128)(2,1)} custom-call(bf16[512,16,128]{2,1,0:T(8,128)(2,1)S(1)} %bitcast.10, f32[2048]{0:T(1024)S(1)} %copy-done.3), custom_call_target="tpu_custom_call" | custom-call | tf_op jit(solution)/shard_map/forward_columns/pallas_call | solution.py:442
  50.8 7.4 %all-to-all-start.1 = ((bf16[128,88,128]{2,1,0:T(8,128)(2,1)}), bf16[128,88,128]{2,1,0:T(8,128)(2,1)}, u32[]{:S(2)}, u32[]{:S(2)}) async-start(bf16[128,88,128]{2,1,0:T(8,128)(2,1)} %forward_columns.1), calls=%async_computation.1 | async-start | bytes 5767168 | tf_op jit(solution)/shard_map/all_to_all | solution.py:554
  58.2 3.5 %sine_select_fusion.twist_ref = f32[128,8,128]{2,1,0:T(8,128)} fusion(s32[128]{0:T(128)S(1)} %get-tuple-element.27, s32[128]{0:T(128)S(1)} %get-tuple-element.30, s32[]{:T(128)S(6)} %mul.28, s32[128]{0:T(128)S(1)} %get-tuple-element.25, s32[128]{0:T(128)S(1)} %get-tuple-element.28, s32[128]{0:T(128)S(1)} %get-tuple-element.26, s32[128]{0:T(128)S(1)} %get-tuple-element.29, ...), kind=kLoop, calls=%fused_computation.6 | loop fusion | flops 3014656 | bytes 527876 | tf_op jit(solution)/shard_map/jit(_where)/select_n | solution.py:415
  61.8 5.2 %twists.1 = (f32[128,5,8,128]{3,2,1,0:T(8,128)}, f32[128,5,8,128]{3,2,1,0:T(8,128)}) custom-call(f32[128,8,128]{2,1,0:T(8,128)} %sine_select_fusion.twist_ref), custom_call_target="tpu_custom_call" | custom-call | flops 8000000 | bytes 6291456 | tf_op jit(solution)/shard_map/twists/pallas_call | solution.py:469
  67.0 0.0 copy-start.5
  67.0 38.9 %collective-permute-done.code_ref = bf16[16,3,136,128]{3,2,1,0:T(8,128)(2,1)} collective-permute-done((bf16[16,3,136,128]{3,2,1,0:T(8,128)(2,1)}, bf16[16,3,136,128]{3,2,1,0:T(8,128)(2,1)}, u32[]{:S(2)}, u32[]{:S(2)}) %collective-permute-start) | collective-permute-done | bytes 1671200 | tf_op jit(solution)/shard_map/ppermute | solution.py:550
  105.8 0.0 copy-start.1
  105.8 10.0 %merge_filters.1 = (f32[8192,128]{1,0:T(8,128)}, f32[8192,128]{1,0:T(8,128)}) custom-call(f32[8192,128]{1,0:T(8,128)} %bitcast.14, f32[8192,128]{1,0:T(8,128)} %bitcast.16, bf16[16,3,136,128]{3,2,1,0:T(8,128)(2,1)} %collective-permute-done.code_ref), custom_call_target="tpu_custom_call" | custom-call | flops 80000000000 | bytes 18874368 | tf_op jit(solution)/shard_map/merge_filters/pallas_call | solution.py:483
  115.8 1.9 all-to-all-done.1.x_ref
  117.8 0.0 copy-done.5
  117.8 0.3 jit_solution_.3.root_ref
  118.1 0.0 copy-done.1
  118.1 16.4 %filter_rows.1 = bf16[128,88,128]{2,1,0:T(8,128)(2,1)} custom-call(bf16[128,88,128]{2,1,0:T(8,128)(2,1)} %all-to-all-done.1.x_ref, f32[128,5,8,128]{3,2,1,0:T(8,128)S(1)} %copy-done.1, f32[128,5,8,128]{3,2,1,0:T(8,128)} %get-tuple-element.17.twist_sin, f32[8192,128]{1,0:T(8,128)} %get-tuple-element.19.filter_real, ...), custom_call_target="tpu_custom_call" | custom-call | tf_op jit(solution)/shard_map/filter_rows/pallas_call | solution.py:497
  134.5 47.8 %all_to_all.33.x_ref = bf16[128,88,128]{2,1,0:T(8,128)(2,1)S(1)} all-to-all(bf16[128,88,128]{2,1,0:T(8,128)(2,1)} %filter_rows.1), channel_id=1, replica_groups=mesh['row'=8,'col'=16] {'row','col'}, dimensions={0} | all-to-all | bytes 5767168 | tf_op jit(solution)/shard_map/all_to_all | solution.py:558
  182.3 7.5 %backward_columns.1 = bf16[8,8,136,128]{3,2,1,0:T(8,128)(2,1)S(1)} custom-call(bf16[128,88,128]{2,1,0:T(8,128)(2,1)S(1)} %all_to_all.33.x_ref, f32[2048]{0:T(1024)S(1)} %copy-done.3), custom_call_target="tpu_custom_call" | custom-call | tf_op jit(solution)/shard_map/backward_columns/pallas_call | solution.py:512
  189.9 0.0 copy-start
  189.9 0.0 copy-start.2
  189.9 0.0 copy-start.4
  189.9 31.0 %all_to_all.34.x_ref = bf16[8,8,136,128]{3,2,1,0:T(8,128)(2,1)S(1)} all-to-all(bf16[8,8,136,128]{3,2,1,0:T(8,128)(2,1)S(1)} %backward_columns.1), channel_id=1, replica_groups=mesh['row'=8,'col'=16] {'row'}, dimensions={0} | all-to-all | bytes 4456448 | tf_op jit(solution)/shard_map/all_to_all | solution.py:560
  220.9 0.0 copy-done
  220.9 0.0 copy-done.2
  220.9 0.0 copy-done.4
  220.9 2.8 %gating.1 = bf16[128,64,128]{2,1,0:T(8,128)(2,1)} custom-call(bf16[8,8,136,128]{3,2,1,0:T(8,128)(2,1)S(1)} %all_to_all.34.x_ref, bf16[128,64,128]{2,1,0:T(8,128)(2,1)S(1)} %copy-done, bf16[128,64,128]{2,1,0:T(8,128)(2,1)S(1)} %copy-done.2, f32[1,128]{1,0:T(1,128)S(1)} %bitcast.12), custom_call_target="tpu_custom_call" | custom-call | tf_op jit(solution)/shard_map/gating/pallas_call | solution.py:524
  (5 shorter events, 0.0 us)
Async XLA Ops:
  3.3 37.1 %all-to-all-start = ((bf16[128,8,8,128]{3,2,0,1:T(8,128)(2,1)}), bf16[128,8,8,128]{3,2,0,1:T(8,128)(2,1)S(1)}, u32[]{:S(2)}, u32[]{:S(2)}) async-start(bf16[128,8,8,128]{3,2,0,1:T(8,128)(2,1)} %copy.9), calls=%async_computation | async-start | bytes 4194304 | tf_op jit(solution)/shard_map/all_to_all | solution.py:548
  9.2 34.0 %copy-start.3 = (f32[2048]{0:T(1024)S(1)}, f32[2048]{0:T(1024)}, u32[]{:S(2)}) copy-start(f32[2048]{0:T(1024)} %constant.72.clone.table_ref) | copy-start | bytes 24580
  40.4 65.5 %collective-permute-start = (bf16[16,3,136,128]{3,2,1,0:T(8,128)(2,1)}, bf16[16,3,136,128]{3,2,1,0:T(8,128)(2,1)}, u32[]{:S(2)}, u32[]{:S(2)}) collective-permute-start(bf16[16,3,136,128]{3,2,1,0:T(8,128)(2,1)} %filter_codes.1), channel_id=1, source_target_pairs={{0,127},{1,126},{2,125},{3,124},{4,123},{5,122},{6,121},{7,120},{8... | collective-permute-start | bytes 5013512 | tf_op jit(solution)/shard_map/ppermute | solution.py:550
  50.8 66.9 %all-to-all-start.1 = ((bf16[128,88,128]{2,1,0:T(8,128)(2,1)}), bf16[128,88,128]{2,1,0:T(8,128)(2,1)}, u32[]{:S(2)}, u32[]{:S(2)}) async-start(bf16[128,88,128]{2,1,0:T(8,128)(2,1)} %forward_columns.1), calls=%async_computation.1 | async-start | bytes 5767168 | tf_op jit(solution)/shard_map/all_to_all | solution.py:554
  67.0 50.8 %copy-start.5 = (f32[2,16,8,8]{3,2,1,0:T(8,128)S(1)}, f32[2,16,8,8]{3,2,1,0:T(8,128)}, u32[]{:S(2)}) copy-start(f32[2,16,8,8]{3,2,1,0:T(8,128)} %constant.73.clone) | copy-start | bytes 24580
  105.8 12.3 %copy-start.1 = (f32[128,5,8,128]{3,2,1,0:T(8,128)S(1)}, f32[128,5,8,128]{3,2,1,0:T(8,128)}, u32[]{:S(2)}) copy-start(f32[128,5,8,128]{3,2,1,0:T(8,128)} %get-tuple-element.16.twist_cos) | copy-start | bytes 7864324
  189.9 31.1 %copy-start = (bf16[128,64,128]{2,1,0:T(8,128)(2,1)S(1)}, bf16[128,64,128]{2,1,0:T(8,128)(2,1)}, u32[]{:S(2)}) copy-start(bf16[128,64,128]{2,1,0:T(8,128)(2,1)} %value_ref.1) | copy-start | bytes 6291460
  189.9 31.1 %copy-start.2 = (bf16[128,64,128]{2,1,0:T(8,128)(2,1)S(1)}, bf16[128,64,128]{2,1,0:T(8,128)(2,1)}, u32[]{:S(2)}) copy-start(bf16[128,64,128]{2,1,0:T(8,128)(2,1)} %gate_ref.1) | copy-start | bytes 6291460
  189.9 31.1 %copy-start.4 = (f32[128]{0:T(128)S(1)}, f32[128]{0:T(128)}, u32[]{:S(2)}) copy-start(f32[128]{0:T(128)} %param.11) | copy-start | bytes 1540

commit v4 on v3

--- a/solution.py
+++ b/solution.py
@@ -195,10 +195,6 @@
     repeat(128, third, TE)
 
 
-def lane(x, k):
-    return jnp.broadcast_to(x[:, k : k + 1], (8, 128))
-
-
 def filter_kernel(re_ref, im_ref, out_ref):
     for s in range(3):
         blocks = []
@@ -210,14 +206,6 @@
             out_ref[0, s, rows, :] = v
 
         encode(blocks, store)
-
-
-def twist_kernel(twist_ref, cos_ref, sin_ref):
-    for a in range(32):
-        tab = twist_ref[a]
-        for i in range(5):
-            cos_ref[a, i] = lane(tab, i)
-            sin_ref[a, i] = lane(tab, 8 + i)
 
 
 def merge_kernel(re_ref, im_ref, code_ref, out_re, out_im, far_re, far_im):
@@ -237,44 +225,32 @@
         out_im[here, :] = im_ref[here, :] - far_im[there, :]
 
 
-def middle_kernel(x_ref, twist_cos, twist_sin, filter_real, filter_imag, root_ref, out_ref,
+def middle_kernel(x_ref, far_ref, near_ref, filter_real, filter_imag, root_ref, out_ref,
                   re_ref, im_ref, re2_ref, im2_ref, tc_ref, ts_ref, fr_ref, fi_ref, sems):
-    parts = []
-    for k in range(4):
-        rows = pl.ds(32 * k, 32)
-        parts.append(
-            [
-                pltpu.make_async_copy(twist_cos.at[rows], tc_ref.at[rows], sems.at[2 * k]),
-                pltpu.make_async_copy(twist_sin.at[rows], ts_ref.at[rows], sems.at[2 * k + 1]),
-            ]
-        )
-    parts.append(
-        [
-            pltpu.make_async_copy(filter_real, fr_ref, sems.at[8]),
-            pltpu.make_async_copy(filter_imag, fi_ref, sems.at[9]),
-        ]
-    )
-    for part in parts:
-        for c in part:
-            c.start()
+    copies = [
+        pltpu.make_async_copy(filter_real, fr_ref, sems.at[0]),
+        pltpu.make_async_copy(filter_imag, fi_ref, sems.at[1]),
+    ]
+    for c in copies:
+        c.start()
 
     def first(src):
         a = 8 * (src % 16) + src // 16
         scale = decode_scale(x_ref[src, 80:88, :])
         for i in range(5):
             x = decode_pair(x_ref[src, 16 * i : 16 * i + 16, :])
-            put(re_ref, im_ref, i, slot(a), times(x, scale * tc_ref[src, i], scale * ts_ref[src, i]))
-
-    for k in range(4):
-        for c in parts[k]:
-            c.wait()
-        repeat(32, lambda src, k=k: first(32 * k + src), TD)
+            c, s = times((near_ref[0, i], near_ref[1, i]), far_ref[16 * src + i], far_ref[16 * src + 8 + i])
+            tc_ref[src, i] = c
+            ts_ref[src, i] = s
+            put(re_ref, im_ref, i, slot(a), times(x, scale * c, scale * s))
+
+    repeat(128, first, TD)
 
     def second(i):
         transform_128(re_ref, im_ref, i, -1)
 
     repeat(5, second)
-    for c in parts[4]:
+    for c in copies:
         c.wait()
 
     def third(e):
@@ -405,17 +381,16 @@
     return np.broadcast_to(both[..., None], (2, 16, 8, 8, 128))
 
 
-def twist_table(device):
-    shape = (128, 8, 128)
-    lanes = lax.broadcasted_iota(jnp.int32, shape, 2)
-    source = lax.broadcasted_iota(jnp.int32, shape, 0)
-    q = 64 * (source % 16) + 8 * (source // 16) + lax.broadcasted_iota(jnp.int32, shape, 1)
-    kp = 8 * device + lanes % 8
-    angle = (q * kp % 1048576).astype(f32) * (-2.0 * math.pi / 1048576.0)
-    return jnp.where(lanes < 8, jnp.cos(angle), jnp.sin(angle))
-
-
-twist_tables = twist_table
+def twist_tables(device):
+    unit = -2.0 * math.pi / 1048576.0
+    source = lax.broadcasted_iota(jnp.int32, (128, 16), 0)
+    i = lax.broadcasted_iota(jnp.int32, (128, 16), 1)
+    angle = ((64 * (source % 16) + 8 * (source // 16)) * (8 * device + i % 8) % 1048576).astype(f32) * unit
+    far = jnp.where(i < 8, jnp.cos(angle), jnp.sin(angle)).reshape(-1)
+    shape = (8, 8, 128)
+    kp = 8 * device + lax.broadcasted_iota(jnp.int32, shape, 0)
+    angle = (kp * lax.broadcasted_iota(jnp.int32, shape, 1)).astype(f32) * unit
+    return far, jnp.stack([jnp.cos(angle), jnp.sin(angle)])
 
 
 def vspec():
@@ -428,10 +403,6 @@
 
 def aspec():
     return pl.BlockSpec(memory_space=pl.ANY)
-
-
-def small_params():
-    return params()
 
 
 def params(mib=56):
@@ -458,24 +429,10 @@
         out_shape=jax.ShapeDtypeStruct((16, 3, 136, 128), bf16),
         in_specs=[rows, rows],
         out_specs=pl.BlockSpec((1, 3, 136, 128), lambda g: (g, 0, 0, 0)),
-        compiler_params=small_params(),
+        compiler_params=params(),
         cost_estimate=pl.CostEstimate(flops=8000000, bytes_accessed=10 << 20, transcendentals=1000000),
         name="filter_codes",
     )(filter_real, filter_imag)
-
-
-def twists(twist):
-    wide = pl.BlockSpec((32, 5, 8, 128), lambda g: (g, 0, 0, 0))
-    return pl.pallas_call(
-        twist_kernel,
-        grid=(4,),
-        out_shape=[jax.ShapeDtypeStruct((128, 5, 8, 128), f32)] * 2,
-        in_specs=[pl.BlockSpec((32, 8, 128), lambda g: (g, 0, 0))],
-        out_specs=[wide, wide],
-        compiler_params=small_params(),
-        cost_estimate=pl.CostEstimate(flops=8000000, bytes_accessed=6 << 20, transcendentals=0),
-        name="twists",
-    )(twist)
 
 
 def merged(filter_real, filter_imag, codes):
@@ -487,25 +444,25 @@
         in_specs=[rows, rows, pl.BlockSpec((2, 3, 136, 128), lambda g: (7 - g, 0, 0, 0))],
         out_specs=[rows, rows],
         scratch_shapes=[pltpu.VMEM((1024, 128), f32)] * 2,
-        compiler_params=small_params(),
+        compiler_params=params(),
         cost_estimate=pl.CostEstimate(flops=80000000000, bytes_accessed=18 << 20, transcendentals=0),
         name="merge_filters",
     )(filter_real, filter_imag, codes)
 
 
-def middle(arrived, twist_cos, twist_sin, filter_real, filter_imag, table):
+def middle(arrived, far, near, filter_real, filter_imag, roots):
     return pl.pallas_call(
         middle_kernel,
         out_shape=jax.ShapeDtypeStruct((128, 88, 128), bf16),
-        in_specs=[vspec()] + [aspec()] * 4 + [vspec()],
+        in_specs=[vspec(), sspec(), vspec(), aspec(), aspec(), vspec()],
         out_specs=vspec(),
-        scratch_shapes=[pltpu.VMEM((8 * STR, 128), f32)] * 4
+        scratch_shapes=[pltpu.VMEM((5 * STR, 128), f32)] * 4
         + [pltpu.VMEM((128, 5, 8, 128), f32)] * 2
         + [pltpu.VMEM((8192, 128), f32)] * 2
-        + [pltpu.SemaphoreType.DMA((10,))],
+        + [pltpu.SemaphoreType.DMA((2,))],
         compiler_params=params(50),
         name="filter_rows",
-    )(arrived, twist_cos, twist_sin, filter_real, filter_imag, table)
+    )(arrived, far, near, filter_real, filter_imag, roots)
 
 
 def backward(returned, table):
@@ -550,11 +507,10 @@
     codes = lax.ppermute(codes, everyone, [(d, 127 - d) for d in range(128)])
     spectrum = forward(columns.reshape(512, 16, 128), table)
     spectrum, device = lax.optimization_barrier((spectrum, device))
-    twist = twist_table(device)
+    far, near = twist_tables(device)
     arrived = lax.all_to_all(spectrum, everyone, split_axis=0, concat_axis=0, tiled=True)
-    twist_cos, twist_sin = twists(twist)
     both_real, both_imag = merged(filter_real, filter_imag, codes)
-    leaving = middle(arrived, twist_cos, twist_sin, both_real, both_imag, jnp.asarray(wide_roots()))
+    leaving = middle(arrived, far, near, both_real, both_imag, jnp.asarray(wide_roots()))
     returned = lax.all_to_all(leaving, everyone, split_axis=0, concat_axis=0, tiled=True)
     convolved = backward(returned, table)
     settled = lax.all_to_all(convolved, "row", split_axis=0, concat_axis=0, tiled=True)

time: 225 us -> 222 us (0.987)
  waiting for transfers between devices: 61.2 us -> 69.4 us
  Pallas kernels: 60.3 us -> 52.7 us
  other arithmetic: 3.53 us -> 0.47 us
    ppermute x1, waiting for transfers between devices: 38.9 us -> 47 us  [convolve(): codes = lax.ppermute(codes, everyone, [(d, 127 - d) for d in range(128)])]
    pallas_call x1 -> x0, Pallas kernels: 5.2 us -> none  [twists(): pl.pallas_call(twist_kernel, grid=(4,), out_shape=[jax.ShapeDtypeStruct((...]
    select_n x1, other arithmetic: 3.5 us -> 0.06 us  [twist_tables(): far = jnp.where(i < 8, jnp.cos(angle), jnp.sin(angle)).reshape(-1)]
  transfers between devices with their start and end apart: 3 -> 3, of which waited for: 3 -> 3; matrix products, arithmetic and copies ran while one was open for 2% -> 0% of each run, Pallas kernels for 15% -> 13%
where the time goes in v4:
time: 222 us; the launch traced here: 221 us
  blocking collectives  78.6 us (35%)
  waiting for transfers between devices  69.4 us (31%)
  Pallas kernels  52.7 us (24%)
  starting transfers between devices  16.1 us (7%)
  local copies, waits for them, and re-layouts  3.84 us (2%)
    all_to_all x1, blocking collectives, convolve(): lax.all_to_all(leaving, everyone, split_axis=0, concat_axis=0, tiled=True)  47.6 us
    ppermute x1, waiting for transfers between devices, convolve(): codes = lax.ppermute(codes, everyone, [(d, 127 - d) for d in range(128)])  47 us
    all_to_all x1, blocking collectives, convolve(): lax.all_to_all(convolved, 'row', split_axis=0, concat_axis=0, tiled=True)  31 us
    all_to_all x1, waiting for transfers between devices, convolve(): lax.all_to_all(pieces, 'row', split_axis=1, concat_axis=0, tiled=True)  20.5 us
    pallas_call x1, Pallas kernels, middle(): pl.pallas_call(middle_kernel, out_shape=jax.ShapeDtypeStruct((128, 88, 12...  14.2 us
    pallas_call x1, Pallas kernels, filter_codes(): pl.pallas_call(filter_kernel, grid=(16,), out_shape=jax.ShapeDtypeStruct(...  10.7 us
    pallas_call x1, Pallas kernels, merged(): pl.pallas_call(merge_kernel, grid=(8,), out_shape=[jax.ShapeDtypeStruct((...  9.87 us
    pallas_call x1, Pallas kernels, forward(): pl.pallas_call(forward_kernel, out_shape=jax.ShapeDtypeStruct((128, 88, 1...  7.61 us
  transfers between devices with their start and end apart: 3, of which 3 were waited for; matrix products, arithmetic and copies ran while one was open for 0% of the time, Pallas kernels for 13%

profile of v4, /device:TPU:0, one launch (start us, length us, event | category | flops | bytes accessed | tf_op | source)
XLA Modules:
  0.0 221.3 jit_solution(11388736459520251793)
XLA Ops:
  0.0 3.3 %copy.10 = bf16[128,8,8,128]{3,2,0,1:T(8,128)(2,1)} copy(bf16[128,8,8,128]{3,2,1,0:T(8,128)(2,1)} %bitcast.11) | data formatting | bytes 4194304 | tf_op jit(solution)/shard_map/reshape | solution.py:503
  3.3 5.9 %all-to-all-start = ((bf16[128,8,8,128]{3,2,0,1:T(8,128)(2,1)}), bf16[128,8,8,128]{3,2,0,1:T(8,128)(2,1)S(1)}, u32[]{:S(2)}, u32[]{:S(2)}) async-start(bf16[128,8,8,128]{3,2,0,1:T(8,128)(2,1)} %copy.10), calls=%async_computation | async-start | bytes 4194304 | tf_op jit(solution)/shard_map/all_to_all | solution.py:505
  9.2 0.0 copy-start.2
  9.2 10.7 %filter_codes.1 = bf16[16,3,136,128]{3,2,1,0:T(8,128)(2,1)} custom-call(f32[8192,128]{1,0:T(8,128)} %bitcast.13, f32[8192,128]{1,0:T(8,128)} %bitcast.15), custom_call_target="tpu_custom_call" | custom-call | flops 8000000 | bytes 10485760 | tf_op jit(solution)/shard_map/filter_codes/pallas_call | solution.py:426
  19.9 20.5 %all-to-all-done = bf16[128,8,8,128]{3,2,0,1:T(8,128)(2,1)S(1)} async-done(((bf16[128,8,8,128]{3,2,0,1:T(8,128)(2,1)}), bf16[128,8,8,128]{3,2,0,1:T(8,128)(2,1)S(1)}, u32[]{:S(2)}, u32[]{:S(2)}) %all-to-all-start) | async-done | bytes 2097184 | tf_op jit(solution)/shard_map/all_to_all | solution.py:505
  40.4 2.8 %collective-permute-start = (bf16[16,3,136,128]{3,2,1,0:T(8,128)(2,1)}, bf16[16,3,136,128]{3,2,1,0:T(8,128)(2,1)}, u32[]{:S(2)}, u32[]{:S(2)}) collective-permute-start(bf16[16,3,136,128]{3,2,1,0:T(8,128)(2,1)} %filter_codes.1), channel_id=1, source_target_pairs={{0,127},{1,126},{2,125},{3,124},{4,123},{5,122},{6,121},{7,120},{8... | collective-permute-start | bytes 5013512 | tf_op jit(solution)/shard_map/ppermute | solution.py:507
  43.2 0.1 iota.47
  43.3 0.0 copy-done.2
  43.4 7.6 %forward_columns.1 = bf16[128,88,128]{2,1,0:T(8,128)(2,1)} custom-call(bf16[512,16,128]{2,1,0:T(8,128)(2,1)S(1)} %bitcast.10, f32[2048]{0:T(1024)S(1)} %copy-done.2), custom_call_target="tpu_custom_call" | custom-call | tf_op jit(solution)/shard_map/forward_columns/pallas_call | solution.py:413
  51.0 7.4 %all-to-all-start.1 = ((bf16[128,88,128]{2,1,0:T(8,128)(2,1)}), bf16[128,88,128]{2,1,0:T(8,128)(2,1)}, u32[]{:S(2)}, u32[]{:S(2)}) async-start(bf16[128,88,128]{2,1,0:T(8,128)(2,1)} %forward_columns.1), calls=%async_computation.1 | async-start | bytes 5767168 | tf_op jit(solution)/shard_map/all_to_all | solution.py:511
  58.4 0.2 add_multiply_fusion
  58.6 0.1 reshape.67
  58.6 0.2 fusion.1
  58.9 0.1 sine_select_fusion.far_ref
  58.9 0.0 copy-start.4
  58.9 47.0 %collective-permute-done.code_ref = bf16[16,3,136,128]{3,2,1,0:T(8,128)(2,1)} collective-permute-done((bf16[16,3,136,128]{3,2,1,0:T(8,128)(2,1)}, bf16[16,3,136,128]{3,2,1,0:T(8,128)(2,1)}, u32[]{:S(2)}, u32[]{:S(2)}) %collective-permute-start) | collective-permute-done | bytes 1671200 | tf_op jit(solution)/shard_map/ppermute | solution.py:507
  105.9 9.9 %merge_filters.1 = (f32[8192,128]{1,0:T(8,128)}, f32[8192,128]{1,0:T(8,128)}) custom-call(f32[8192,128]{1,0:T(8,128)} %bitcast.14, f32[8192,128]{1,0:T(8,128)} %bitcast.16, bf16[16,3,136,128]{3,2,1,0:T(8,128)(2,1)} %collective-permute-done.code_ref), custom_call_target="tpu_custom_call" | custom-call | flops 80000000000 | bytes 18874368 | tf_op jit(solution)/shard_map/merge_filters/pallas_call | solution.py:440
  115.8 2.0 all-to-all-done.1.x_ref
  117.8 0.0 copy-done.4
  117.8 0.3 jit_solution_.3.root_ref
  118.1 14.2 %filter_rows.1 = bf16[128,88,128]{2,1,0:T(8,128)(2,1)S(1)} custom-call(bf16[128,88,128]{2,1,0:T(8,128)(2,1)} %all-to-all-done.1.x_ref, f32[2048]{0:T(1024)S(1)} %sine_select_fusion.far_ref, f32[2,8,8,128]{3,2,1,0:T(8,128)S(1)} %pad_maximum_fusion.near_ref, f32[8192,128]{1,0:T(8,128)} %get-tuple-element.15.filter_real, ...), custom_call_target="tpu_custom_call" | custom-call | tf_op jit(solution)/shard_map/filter_rows/pallas_call | solution.py:454
  132.4 47.6 %all_to_all.33.x_ref = bf16[128,88,128]{2,1,0:T(8,128)(2,1)S(1)} all-to-all(bf16[128,88,128]{2,1,0:T(8,128)(2,1)S(1)} %filter_rows.1), channel_id=1, replica_groups=mesh['row'=8,'col'=16] {'row','col'}, dimensions={0} | all-to-all | bytes 5767168 | tf_op jit(solution)/shard_map/all_to_all | solution.py:514
  180.0 7.5 %backward_columns.1 = bf16[8,8,136,128]{3,2,1,0:T(8,128)(2,1)S(1)} custom-call(bf16[128,88,128]{2,1,0:T(8,128)(2,1)S(1)} %all_to_all.33.x_ref, f32[2048]{0:T(1024)S(1)} %copy-done.2), custom_call_target="tpu_custom_call" | custom-call | tf_op jit(solution)/shard_map/backward_columns/pallas_call | solution.py:469
  187.5 0.0 copy-start
  187.5 0.0 copy-start.1
  187.5 0.0 copy-start.3
  187.5 31.0 %all_to_all.34.x_ref = bf16[8,8,136,128]{3,2,1,0:T(8,128)(2,1)S(1)} all-to-all(bf16[8,8,136,128]{3,2,1,0:T(8,128)(2,1)S(1)} %backward_columns.1), channel_id=1, replica_groups=mesh['row'=8,'col'=16] {'row'}, dimensions={0} | all-to-all | bytes 4456448 | tf_op jit(solution)/shard_map/all_to_all | solution.py:516
  218.5 0.0 copy-done
  218.6 0.0 copy-done.1
  218.6 0.0 copy-done.3
  218.6 2.8 %gating.1 = bf16[128,64,128]{2,1,0:T(8,128)(2,1)} custom-call(bf16[8,8,136,128]{3,2,1,0:T(8,128)(2,1)S(1)} %all_to_all.34.x_ref, bf16[128,64,128]{2,1,0:T(8,128)(2,1)S(1)} %copy-done, bf16[128,64,128]{2,1,0:T(8,128)(2,1)S(1)} %copy-done.1, f32[1,128]{1,0:T(1,128)S(1)} %bitcast.12), custom_call_target="tpu_custom_call" | custom-call | tf_op jit(solution)/shard_map/gating/pallas_call | solution.py:481
  (9 shorter events, 0.1 us)
Async XLA Ops:
  3.3 37.1 %all-to-all-start = ((bf16[128,8,8,128]{3,2,0,1:T(8,128)(2,1)}), bf16[128,8,8,128]{3,2,0,1:T(8,128)(2,1)S(1)}, u32[]{:S(2)}, u32[]{:S(2)}) async-start(bf16[128,8,8,128]{3,2,0,1:T(8,128)(2,1)} %copy.10), calls=%async_computation | async-start | bytes 4194304 | tf_op jit(solution)/shard_map/all_to_all | solution.py:505
  9.2 34.1 %copy-start.2 = (f32[2048]{0:T(1024)S(1)}, f32[2048]{0:T(1024)}, u32[]{:S(2)}) copy-start(f32[2048]{0:T(1024)} %constant.73.clone.table_ref) | copy-start | bytes 24580
  40.4 65.5 %collective-permute-start = (bf16[16,3,136,128]{3,2,1,0:T(8,128)(2,1)}, bf16[16,3,136,128]{3,2,1,0:T(8,128)(2,1)}, u32[]{:S(2)}, u32[]{:S(2)}) collective-permute-start(bf16[16,3,136,128]{3,2,1,0:T(8,128)(2,1)} %filter_codes.1), channel_id=1, source_target_pairs={{0,127},{1,126},{2,125},{3,124},{4,123},{5,122},{6,121},{7,120},{8... | collective-permute-start | bytes 5013512 | tf_op jit(solution)/shard_map/ppermute | solution.py:507
  51.0 66.8 %all-to-all-start.1 = ((bf16[128,88,128]{2,1,0:T(8,128)(2,1)}), bf16[128,88,128]{2,1,0:T(8,128)(2,1)}, u32[]{:S(2)}, u32[]{:S(2)}) async-start(bf16[128,88,128]{2,1,0:T(8,128)(2,1)} %forward_columns.1), calls=%async_computation.1 | async-start | bytes 5767168 | tf_op jit(solution)/shard_map/all_to_all | solution.py:511
  58.9 58.8 %copy-start.4 = (f32[2,16,8,8]{3,2,1,0:T(8,128)S(1)}, f32[2,16,8,8]{3,2,1,0:T(8,128)}, u32[]{:S(2)}) copy-start(f32[2,16,8,8]{3,2,1,0:T(8,128)} %constant.74.clone) | copy-start | bytes 24580
  187.5 31.1 %copy-start = (bf16[128,64,128]{2,1,0:T(8,128)(2,1)S(1)}, bf16[128,64,128]{2,1,0:T(8,128)(2,1)}, u32[]{:S(2)}) copy-start(bf16[128,64,128]{2,1,0:T(8,128)(2,1)} %value_ref.1) | copy-start | bytes 6291460
  187.5 31.1 %copy-start.1 = (bf16[128,64,128]{2,1,0:T(8,128)(2,1)S(1)}, bf16[128,64,128]{2,1,0:T(8,128)(2,1)}, u32[]{:S(2)}) copy-start(bf16[128,64,128]{2,1,0:T(8,128)(2,1)} %gate_ref.1) | copy-start | bytes 6291460
  187.5 31.1 %copy-start.3 = (f32[128]{0:T(128)S(1)}, f32[128]{0:T(128)}, u32[]{:S(2)}) copy-start(f32[128]{0:T(128)} %param.11) | copy-start | bytes 1540

commit v5 on v4

--- a/solution.py
+++ b/solution.py
@@ -10,6 +10,7 @@
 
 GS = 2
 TG = 4
+LV = 56
 TM = 1
 TE = 16
 TD = 16
@@ -195,30 +196,50 @@
     repeat(128, third, TE)
 
 
-def filter_kernel(re_ref, im_ref, out_ref):
-    for s in range(3):
-        blocks = []
-        for u in range(8):
-            rows = pl.ds(64 * u + 7 - s, 8, stride=8)
-            blocks += [re_ref[rows, :], im_ref[rows, :]]
-
-        def store(rows, v):
-            out_ref[0, s, rows, :] = v
-
-        encode(blocks, store)
+def leave_kernel(value_hbm, real_hbm, imag_hbm, out_ref, code_ref, value_ref, re_ref, im_ref, sems):
+    copies = [pltpu.make_async_copy(value_hbm, value_ref, sems.at[0])]
+    for g in range(8):
+        rows = pl.ds(1024 * g, 1024)
+        copies.append(pltpu.make_async_copy(real_hbm.at[rows], re_ref.at[rows], sems.at[1 + g]))
+        copies.append(pltpu.make_async_copy(imag_hbm.at[rows], im_ref.at[rows], sems.at[9 + g]))
+    for c in copies:
+        c.start()
+    copies[0].wait()
+
+    def first(k):
+        for pair in range(4):
+            rows = slice(16 * pair, 16 * pair + 16)
+            low, high = value_ref[2 * k, rows, :].astype(f32), value_ref[2 * k + 1, rows, :].astype(f32)
+            for odd in range(2):
+                half = slice(8 * odd, 8 * odd + 8)
+                out_ref[2 * pair + odd, k] = jnp.concatenate([low[half], high[half]], axis=0).astype(bf16)
+
+    repeat(64, first, 8)
+    for g in range(8):
+        copies[1 + 2 * g].wait()
+        copies[2 + 2 * g].wait()
+        for s in range(3):
+            blocks = []
+            for u in range(16):
+                rows = pl.ds(1024 * g + 64 * u + 7 - s, 8, stride=8)
+                blocks += [re_ref[rows, :], im_ref[rows, :]]
+
+            def store(rows, v, g=g, s=s):
+                code_ref[g, s, rows, :] = v
+
+            encode(blocks, store)
 
 
 def merge_kernel(re_ref, im_ref, code_ref, out_re, out_im, far_re, far_im):
     far_re[...] = jnp.zeros((1024, 128), f32)
     far_im[...] = jnp.zeros((1024, 128), f32)
-    for g in range(2):
-        for s in range(3):
-            scale = decode_scale(code_ref[g, s, 128:136, :])
-            for u in range(8):
-                lre, lim = decode_pair(code_ref[g, s, 16 * u : 16 * u + 16, :])
-                rows = pl.ds(512 * g + 64 * u + s + 1, 8, stride=8)
-                far_re[rows, :] = lre * scale
-                far_im[rows, :] = lim * scale
+    for s in range(3):
+        scale = decode_scale(code_ref[0, s, 256:264, :])
+        for u in range(16):
+            lre, lim = decode_pair(code_ref[0, s, 16 * u : 16 * u + 16, :])
+            rows = pl.ds(64 * u + s + 1, 8, stride=8)
+            far_re[rows, :] = lre * scale
+            far_im[rows, :] = lim * scale
     for t in range(128):
         here, there = slice(8 * t, 8 * t + 8), slice(1016 - 8 * t, 1024 - 8 * t)
         out_re[here, :] = re_ref[here, :] + far_re[there, :]
@@ -335,27 +356,27 @@
     repeat(128, third)
 
     def fourth(step):
-        r, g = step // 8, step % 8
-        blocks = [conv_ref[r, 16 * g + k] * (1.0 / 1048576.0) for k in range(16)]
+        r, g = step // 4, step % 4
+        blocks = [conv_ref[r, 32 * g + k] * (1.0 / 1048576.0) for k in range(32)]
 
         def store(rows, v):
             out_ref[r, g, rows, :] = v
 
         encode(blocks, store)
 
-    repeat(64, fourth, TE)
+    repeat(32, fourth, 8)
 
 
 def gate_kernel(x_ref, value_ref, gate_ref, skip_ref, out_ref):
     skip = skip_ref[0:1, :]
 
     def body(at):
-        g, k = at // 8, at % 8
+        g, k = at // 16, at % 16
         start = pl.multiple_of(16 * k, 16)
         for pair in range(4):
             sides = []
             for r in (2 * pair, 2 * pair + 1):
-                scale = decode_scale(x_ref[r, g, 128:136, :])
+                scale = decode_scale(x_ref[r, g, 256:264, :])
                 low, high = decode_pair(x_ref[r, g, pl.ds(start, 16), :])
                 sides.append((low * scale, high * scale))
             for odd in range(2):
@@ -421,18 +442,19 @@
     )(columns, table)
 
 
-def filter_codes(filter_real, filter_imag):
-    rows = pl.BlockSpec((512, 128), lambda g: (g, 0))
+def leave(value, filter_real, filter_imag):
     return pl.pallas_call(
-        filter_kernel,
-        grid=(16,),
-        out_shape=jax.ShapeDtypeStruct((16, 3, 136, 128), bf16),
-        in_specs=[rows, rows],
-        out_specs=pl.BlockSpec((1, 3, 136, 128), lambda g: (g, 0, 0, 0)),
-        compiler_params=params(),
-        cost_estimate=pl.CostEstimate(flops=8000000, bytes_accessed=10 << 20, transcendentals=1000000),
-        name="filter_codes",
-    )(filter_real, filter_imag)
+        leave_kernel,
+        out_shape=[jax.ShapeDtypeStruct((8, 64, 16, 128), bf16), jax.ShapeDtypeStruct((8, 3, 264, 128), bf16)],
+        in_specs=[aspec()] * 3,
+        out_specs=[vspec()] * 2,
+        scratch_shapes=[pltpu.VMEM((128, 64, 128), bf16)]
+        + [pltpu.VMEM((8192, 128), f32)] * 2
+        + [pltpu.SemaphoreType.DMA((17,))],
+        compiler_params=params(LV),
+        cost_estimate=pl.CostEstimate(flops=8000000, bytes_accessed=14 << 20, transcendentals=1000000),
+        name="leave",
+    )(value, filter_real, filter_imag)
 
 
 def merged(filter_real, filter_imag, codes):
@@ -441,7 +463,7 @@
         merge_kernel,
         grid=(8,),
         out_shape=[jax.ShapeDtypeStruct((8192, 128), f32)] * 2,
-        in_specs=[rows, rows, pl.BlockSpec((2, 3, 136, 128), lambda g: (7 - g, 0, 0, 0))],
+        in_specs=[rows, rows, pl.BlockSpec((1, 3, 264, 128), lambda g: (7 - g, 0, 0, 0))],
         out_specs=[rows, rows],
         scratch_shapes=[pltpu.VMEM((1024, 128), f32)] * 2,
         compiler_params=params(),
@@ -468,7 +490,7 @@
 def backward(returned, table):
     return pl.pallas_call(
         backward_kernel,
-        out_shape=jax.ShapeDtypeStruct((8, 8, 136, 128), bf16),
+        out_shape=jax.ShapeDtypeStruct((8, 4, 264, 128), bf16),
         in_specs=[vspec(), sspec()],
         out_specs=vspec(),
         scratch_shapes=[pltpu.VMEM((5 * STR, 128), f32)] * 2 + [pltpu.VMEM((8, 128, 8, 128), f32)],
@@ -483,7 +505,7 @@
         grid=(GS,),
         out_shape=jax.ShapeDtypeStruct((128, 64, 128), bf16),
         in_specs=[
-            pl.BlockSpec((8, 8 // GS, 136, 128), lambda g: (0, g, 0, 0)),
+            pl.BlockSpec((8, 4 // GS, 264, 128), lambda g: (0, g, 0, 0)),
             pl.BlockSpec((128 // GS, 64, 128), lambda g: (g, 0, 0)),
             pl.BlockSpec((128 // GS, 64, 128), lambda g: (g, 0, 0)),
             pl.BlockSpec((1, 128), lambda g: (0, 0)),
@@ -500,9 +522,8 @@
     table = jnp.asarray(roots_table(1024))
     filter_real = filter_real.reshape(8192, 128)
     filter_imag = filter_imag.reshape(8192, 128)
-    pieces = value.reshape(128, 8, 8, 128)
-    codes = filter_codes(filter_real, filter_imag)
-    columns = lax.all_to_all(pieces, "row", split_axis=1, concat_axis=0, tiled=True)
+    pieces, codes = leave(value, filter_real, filter_imag)
+    columns = lax.all_to_all(pieces, "row", split_axis=0, concat_axis=0, tiled=True)
     columns, codes = lax.optimization_barrier((columns, codes))
     codes = lax.ppermute(codes, everyone, [(d, 127 - d) for d in range(128)])
     spectrum = forward(columns.reshape(512, 16, 128), table)

time: 222 us -> 219 us (0.986)
  blocking collectives: 78.6 us -> 110 us
  waiting for transfers between devices: 69.4 us -> 48.3 us
  starting transfers between devices: 16.1 us -> 10.8 us
  Pallas kernels: 52.7 us -> 47.9 us
  local copies, waits for them, and re-layouts: 3.84 us -> 0.55 us
    all_to_all x0 -> x1, blocking collectives: none -> 32.6 us  [convolve(): lax.all_to_all(pieces, 'row', split_axis=0, concat_axis=0, tiled=True)]
    all_to_all x1 -> x0, waiting for transfers between devices: 20.5 us -> none  [convolve(): lax.all_to_all(pieces, 'row', split_axis=1, concat_axis=0, tiled=True)]
    all_to_all x1 -> x0, starting transfers between devices: 5.91 us -> none  [convolve(): lax.all_to_all(pieces, 'row', split_axis=1, concat_axis=0, tiled=True)]
    pallas_call x2, Pallas kernels: 18.2 us -> 13.4 us  [the longest x1 7.44 us: backward(): pl.pallas_call(backward_kernel, out_shape=jax.ShapeDtypeStruct((8, 4, 264...]
    reshape x1 -> x0, local copies, waits for them, and re-layouts: 3.29 us -> none  [convolve(): pieces = value.reshape(128, 8, 8, 128)]
  transfers between devices with their start and end apart: 3 -> 2, of which waited for: 3 -> 2; matrix products, arithmetic and copies ran while one was open for 0% -> 0% of each run, Pallas kernels for 13% -> 8%
where the time goes in v5:
time: 219 us
  blocking collectives  110 us (50%)
  waiting for transfers between devices  48.3 us (22%)
  Pallas kernels  47.9 us (22%)
  starting transfers between devices  10.8 us (5%)
    all_to_all x1, blocking collectives, convolve(): lax.all_to_all(leaving, everyone, split_axis=0, concat_axis=0, tiled=True)  47.2 us
    ppermute x1, waiting for transfers between devices, convolve(): codes = lax.ppermute(codes, everyone, [(d, 127 - d) for d in range(128)])  45.1 us
    all_to_all x1, blocking collectives, convolve(): lax.all_to_all(pieces, 'row', split_axis=0, concat_axis=0, tiled=True)  32.6 us
    all_to_all x1, blocking collectives, convolve(): lax.all_to_all(convolved, 'row', split_axis=0, concat_axis=0, tiled=True)  30.6 us
    pallas_call x1, Pallas kernels, middle(): pl.pallas_call(middle_kernel, out_shape=jax.ShapeDtypeStruct((128, 88, 12...  14.2 us
    pallas_call x1, Pallas kernels, merged(): pl.pallas_call(merge_kernel, grid=(8,), out_shape=[jax.ShapeDtypeStruct((...  9.88 us
    pallas_call x1, Pallas kernels, forward(): pl.pallas_call(forward_kernel, out_shape=jax.ShapeDtypeStruct((128, 88, 1...  7.6 us
    pallas_call x1, Pallas kernels, backward(): pl.pallas_call(backward_kernel, out_shape=jax.ShapeDtypeStruct((8, 4, 264...  7.44 us
  transfers between devices with their start and end apart: 2, of which 2 were waited for; matrix products, arithmetic and copies ran while one was open for 0% of the time, Pallas kernels for 8%

profile of v5, /device:TPU:0, one launch (start us, length us, event | category | flops | bytes accessed | tf_op | source)
XLA Modules:
  0.0 218.6 jit_solution(6325708859188738167)
XLA Ops:
  0.0 6.0 %leave.1 = (bf16[8,64,16,128]{3,2,1,0:T(8,128)(2,1)}, bf16[8,3,264,128]{3,2,1,0:T(8,128)(2,1)}) custom-call(bf16[128,64,128]{2,1,0:T(8,128)(2,1)} %value_ref.1, f32[8192,128]{1,0:T(8,128)} %bitcast.6, f32[8192,128]{1,0:T(8,128)} %bitcast.8), custom_call_target="tpu_custom_call" | custom-call | flops 8000000 | bytes 14680064 | tf_op jit(solution)/shard_map/leave/pallas_call | solution.py:446
  6.0 0.0 copy-start.2
  6.0 32.6 %all_to_all.20 = bf16[8,64,16,128]{3,2,1,0:T(8,128)(2,1)S(1)} all-to-all(bf16[8,64,16,128]{3,2,1,0:T(8,128)(2,1)} %get-tuple-element.13), channel_id=1, replica_groups=mesh['row'=8,'col'=16] {'row'}, dimensions={0} | all-to-all | bytes 4194304 | tf_op jit(solution)/shard_map/all_to_all | solution.py:526
  38.6 4.6 %collective-permute-start = (bf16[8,3,264,128]{3,2,1,0:T(8,128)(2,1)}, bf16[8,3,264,128]{3,2,1,0:T(8,128)(2,1)}, u32[]{:S(2)}, u32[]{:S(2)}) collective-permute-start(bf16[8,3,264,128]{3,2,1,0:T(8,128)(2,1)} %get-tuple-element.18), channel_id=1, source_target_pairs={{0,127},{1,126},{2,125},{3,124},{4,123},{5,122},{6,121},{7,120},{8... | collective-permute-start | bytes 4866056 | tf_op jit(solution)/shard_map/ppermute | solution.py:528
  43.2 0.1 iota.47
  43.3 0.0 copy-done.2
  43.3 7.6 %forward_columns.1 = bf16[128,88,128]{2,1,0:T(8,128)(2,1)} custom-call(bf16[512,16,128]{2,1,0:T(8,128)(2,1)S(1)} %bitcast.4, f32[2048]{0:T(1024)S(1)} %copy-done.2), custom_call_target="tpu_custom_call" | custom-call | tf_op jit(solution)/shard_map/forward_columns/pallas_call | solution.py:434
  50.9 6.2 %all-to-all-start.1 = ((bf16[128,88,128]{2,1,0:T(8,128)(2,1)}), bf16[128,88,128]{2,1,0:T(8,128)(2,1)}, u32[]{:S(2)}, u32[]{:S(2)}) async-start(bf16[128,88,128]{2,1,0:T(8,128)(2,1)} %forward_columns.1), calls=%async_computation.1 | async-start | bytes 5767168 | tf_op jit(solution)/shard_map/all_to_all | solution.py:532
  57.2 0.2 add_multiply_fusion
  57.3 0.1 reshape.63
  57.4 0.2 fusion.1
  57.7 0.1 sine_select_fusion.far_ref
  57.7 0.0 copy-start.4
  57.7 45.1 %collective-permute-done.code_ref = bf16[8,3,264,128]{3,2,1,0:T(8,128)(2,1)} collective-permute-done((bf16[8,3,264,128]{3,2,1,0:T(8,128)(2,1)}, bf16[8,3,264,128]{3,2,1,0:T(8,128)(2,1)}, u32[]{:S(2)}, u32[]{:S(2)}) %collective-permute-start) | collective-permute-done | bytes 1622048 | tf_op jit(solution)/shard_map/ppermute | solution.py:528
  102.8 9.9 %merge_filters.1 = (f32[8192,128]{1,0:T(8,128)}, f32[8192,128]{1,0:T(8,128)}) custom-call(f32[8192,128]{1,0:T(8,128)} %bitcast.7, f32[8192,128]{1,0:T(8,128)} %bitcast.9, bf16[8,3,264,128]{3,2,1,0:T(8,128)(2,1)} %collective-permute-done.code_ref), custom_call_target="tpu_custom_call" | custom-call | flops 80000000000 | bytes 18874368 | tf_op jit(solution)/shard_map/merge_filters/pallas_call | solution.py:462
  112.7 3.2 %all-to-all-done.1.x_ref = bf16[128,88,128]{2,1,0:T(8,128)(2,1)} async-done(((bf16[128,88,128]{2,1,0:T(8,128)(2,1)}), bf16[128,88,128]{2,1,0:T(8,128)(2,1)}, u32[]{:S(2)}, u32[]{:S(2)}) %all-to-all-start.1) | async-done | bytes 2883616 | tf_op jit(solution)/shard_map/all_to_all | solution.py:532
  115.9 0.0 copy-done.4
  115.9 0.3 jit_solution_.3.root_ref
  116.2 14.2 %filter_rows.1 = bf16[128,88,128]{2,1,0:T(8,128)(2,1)S(1)} custom-call(bf16[128,88,128]{2,1,0:T(8,128)(2,1)} %all-to-all-done.1.x_ref, f32[2048]{0:T(1024)S(1)} %sine_select_fusion.far_ref, f32[2,8,8,128]{3,2,1,0:T(8,128)S(1)} %pad_maximum_fusion.near_ref, f32[8192,128]{1,0:T(8,128)} %get-tuple-element.19.filter_real, ...), custom_call_target="tpu_custom_call" | custom-call | tf_op jit(solution)/shard_map/filter_rows/pallas_call | solution.py:476
  130.5 47.2 %all_to_all.21.x_ref = bf16[128,88,128]{2,1,0:T(8,128)(2,1)S(1)} all-to-all(bf16[128,88,128]{2,1,0:T(8,128)(2,1)S(1)} %filter_rows.1), channel_id=1, replica_groups=mesh['row'=8,'col'=16] {'row','col'}, dimensions={0} | all-to-all | bytes 5767168 | tf_op jit(solution)/shard_map/all_to_all | solution.py:535
  177.7 7.4 %backward_columns.1 = bf16[8,4,264,128]{3,2,1,0:T(8,128)(2,1)S(1)} custom-call(bf16[128,88,128]{2,1,0:T(8,128)(2,1)S(1)} %all_to_all.21.x_ref, f32[2048]{0:T(1024)S(1)} %copy-done.2), custom_call_target="tpu_custom_call" | custom-call | tf_op jit(solution)/shard_map/backward_columns/pallas_call | solution.py:491
  185.1 0.0 copy-start
  185.2 0.0 copy-start.1
  185.2 0.0 copy-start.3
  185.2 30.6 %all_to_all.22.x_ref = bf16[8,4,264,128]{3,2,1,0:T(8,128)(2,1)S(1)} all-to-all(bf16[8,4,264,128]{3,2,1,0:T(8,128)(2,1)S(1)} %backward_columns.1), channel_id=1, replica_groups=mesh['row'=8,'col'=16] {'row'}, dimensions={0} | all-to-all | bytes 4325376 | tf_op jit(solution)/shard_map/all_to_all | solution.py:537
  215.8 0.0 copy-done
  215.8 0.0 copy-done.1
  215.8 0.0 copy-done.3
  215.8 2.8 %gating.1 = bf16[128,64,128]{2,1,0:T(8,128)(2,1)} custom-call(bf16[8,4,264,128]{3,2,1,0:T(8,128)(2,1)S(1)} %all_to_all.22.x_ref, bf16[128,64,128]{2,1,0:T(8,128)(2,1)S(1)} %copy-done, bf16[128,64,128]{2,1,0:T(8,128)(2,1)S(1)} %copy-done.1, f32[1,128]{1,0:T(1,128)S(1)} %bitcast.5), custom_call_target="tpu_custom_call" | custom-call | tf_op jit(solution)/shard_map/gating/pallas_call | solution.py:503
  (9 shorter events, 0.1 us)
Async XLA Ops:
  6.0 37.3 %copy-start.2 = (f32[2048]{0:T(1024)S(1)}, f32[2048]{0:T(1024)}, u32[]{:S(2)}) copy-start(f32[2048]{0:T(1024)} %constant.73.clone.table_ref) | copy-start | bytes 24580
  38.6 64.3 %collective-permute-start = (bf16[8,3,264,128]{3,2,1,0:T(8,128)(2,1)}, bf16[8,3,264,128]{3,2,1,0:T(8,128)(2,1)}, u32[]{:S(2)}, u32[]{:S(2)}) collective-permute-start(bf16[8,3,264,128]{3,2,1,0:T(8,128)(2,1)} %get-tuple-element.18), channel_id=1, source_target_pairs={{0,127},{1,126},{2,125},{3,124},{4,123},{5,122},{6,121},{7,120},{8... | collective-permute-start | bytes 4866056 | tf_op jit(solution)/shard_map/ppermute | solution.py:528
  50.9 64.9 %all-to-all-start.1 = ((bf16[128,88,128]{2,1,0:T(8,128)(2,1)}), bf16[128,88,128]{2,1,0:T(8,128)(2,1)}, u32[]{:S(2)}, u32[]{:S(2)}) async-start(bf16[128,88,128]{2,1,0:T(8,128)(2,1)} %forward_columns.1), calls=%async_computation.1 | async-start | bytes 5767168 | tf_op jit(solution)/shard_map/all_to_all | solution.py:532
  57.7 58.2 %copy-start.4 = (f32[2,16,8,8]{3,2,1,0:T(8,128)S(1)}, f32[2,16,8,8]{3,2,1,0:T(8,128)}, u32[]{:S(2)}) copy-start(f32[2,16,8,8]{3,2,1,0:T(8,128)} %constant.74.clone) | copy-start | bytes 24580
  185.1 30.6 %copy-start = (bf16[128,64,128]{2,1,0:T(8,128)(2,1)S(1)}, bf16[128,64,128]{2,1,0:T(8,128)(2,1)}, u32[]{:S(2)}) copy-start(bf16[128,64,128]{2,1,0:T(8,128)(2,1)} %value_ref.1) | copy-start | bytes 6291460
  185.2 30.6 %copy-start.1 = (bf16[128,64,128]{2,1,0:T(8,128)(2,1)S(1)}, bf16[128,64,128]{2,1,0:T(8,128)(2,1)}, u32[]{:S(2)}) copy-start(bf16[128,64,128]{2,1,0:T(8,128)(2,1)} %gate_ref.1) | copy-start | bytes 6291460
  185.2 30.6 %copy-start.3 = (f32[128]{0:T(128)S(1)}, f32[128]{0:T(128)}, u32[]{:S(2)}) copy-start(f32[128]{0:T(128)} %param.11) | copy-start | bytes 1540

commit v6 on v5

--- a/solution.py
+++ b/solution.py
@@ -137,6 +137,23 @@
     return 17 * (k % 8) + k // 8
 
 
+def send_parts(step, count, together, src_ref, dst_ref, sems):
+    size = src_ref.shape[0] // 4
+
+    def copy(k):
+        rows = pl.ds(size * k, size)
+        return pltpu.make_async_copy(src_ref.at[rows], dst_ref.at[rows], sems.at[k])
+
+    def part(k, carry):
+        repeat(count // 4, lambda n: step(count // 4 * k + n), together)
+        copy(k).start()
+        return carry
+
+    lax.fori_loop(0, 4, part, 0)
+    for k in range(4):
+        copy(k).wait()
+
+
 def encode(blocks, store):
     tops = [jnp.abs(x) for x in blocks]
     while len(tops) > 1:
@@ -158,7 +175,7 @@
     return logs[0:8], logs[8:16]
 
 
-def forward_kernel(x_ref, table_ref, out_ref, re_ref, im_ref):
+def forward_kernel(x_ref, table_ref, out_hbm, re_ref, im_ref, out_ref, sems):
     def first(pair):
         both = [x_ref[64 * r + pair].astype(f32) for r in range(8)]
         for odd in range(2):
@@ -193,7 +210,7 @@
 
         encode(blocks, store)
 
-    repeat(128, third, TE)
+    send_parts(third, 128, TE, out_ref, out_hbm, sems)
 
 
 def leave_kernel(value_hbm, real_hbm, imag_hbm, out_ref, code_ref, value_ref, re_ref, im_ref, sems):
@@ -246,8 +263,8 @@
         out_im[here, :] = im_ref[here, :] - far_im[there, :]
 
 
-def middle_kernel(x_ref, far_ref, near_ref, filter_real, filter_imag, root_ref, out_ref,
-                  re_ref, im_ref, re2_ref, im2_ref, tc_ref, ts_ref, fr_ref, fi_ref, sems):
+def middle_kernel(x_ref, far_ref, near_ref, filter_real, filter_imag, root_ref, out_hbm,
+                  re_ref, im_ref, re2_ref, im2_ref, tc_ref, ts_ref, fr_ref, fi_ref, out_ref, sems, out_sems):
     copies = [
         pltpu.make_async_copy(filter_real, fr_ref, sems.at[0]),
         pltpu.make_async_copy(filter_imag, fi_ref, sems.at[1]),
@@ -314,10 +331,10 @@
 
         encode(blocks, store)
 
-    repeat(128, fifth, TE)
-
-
-def backward_kernel(x_ref, table_ref, out_ref, re_ref, im_ref, conv_ref):
+    send_parts(fifth, 128, TE, out_ref, out_hbm, out_sems)
+
+
+def backward_kernel(x_ref, table_ref, out_hbm, re_ref, im_ref, conv_ref, out_ref, sems):
     def first(d):
         scale = decode_scale(x_ref[d, 80:88, :])
         for i in range(5):
@@ -364,7 +381,7 @@
 
         encode(blocks, store)
 
-    repeat(32, fourth, 8)
+    send_parts(fourth, 32, 8, out_ref, out_hbm, sems)
 
 
 def gate_kernel(x_ref, value_ref, gate_ref, skip_ref, out_ref):
@@ -435,8 +452,9 @@
         forward_kernel,
         out_shape=jax.ShapeDtypeStruct((128, 88, 128), bf16),
         in_specs=[vspec(), sspec()],
-        out_specs=vspec(),
-        scratch_shapes=[pltpu.VMEM((5 * STR, 128), f32)] * 2,
+        out_specs=aspec(),
+        scratch_shapes=[pltpu.VMEM((5 * STR, 128), f32)] * 2
+        + [pltpu.VMEM((128, 88, 128), bf16), pltpu.SemaphoreType.DMA((4,))],
         compiler_params=params(16),
         name="forward_columns",
     )(columns, table)
@@ -477,11 +495,12 @@
         middle_kernel,
         out_shape=jax.ShapeDtypeStruct((128, 88, 128), bf16),
         in_specs=[vspec(), sspec(), vspec(), aspec(), aspec(), vspec()],
-        out_specs=vspec(),
+        out_specs=aspec(),
         scratch_shapes=[pltpu.VMEM((5 * STR, 128), f32)] * 4
         + [pltpu.VMEM((128, 5, 8, 128), f32)] * 2
         + [pltpu.VMEM((8192, 128), f32)] * 2
-        + [pltpu.SemaphoreType.DMA((2,))],
+        + [pltpu.VMEM((128, 88, 128), bf16)]
+        + [pltpu.SemaphoreType.DMA((2,)), pltpu.SemaphoreType.DMA((4,))],
         compiler_params=params(50),
         name="filter_rows",
     )(arrived, far, near, filter_real, filter_imag, roots)
@@ -492,8 +511,9 @@
         backward_kernel,
         out_shape=jax.ShapeDtypeStruct((8, 4, 264, 128), bf16),
         in_specs=[vspec(), sspec()],
-        out_specs=vspec(),
-        scratch_shapes=[pltpu.VMEM((5 * STR, 128), f32)] * 2 + [pltpu.VMEM((8, 128, 8, 128), f32)],
+        out_specs=aspec(),
+        scratch_shapes=[pltpu.VMEM((5 * STR, 128), f32)] * 2 + [pltpu.VMEM((8, 128, 8, 128), f32)]
+        + [pltpu.VMEM((8, 4, 264, 128), bf16), pltpu.SemaphoreType.DMA((4,))],
         compiler_params=params(24),
         name="backward_columns",
     )(returned, table)

time: 219 us -> 221 us (level)
  no operation moved by 1% of the time
where the time goes in v6:
time: 221 us; the launch traced here: 220 us
  blocking collectives  110 us (50%)
  waiting for transfers between devices  49 us (22%)
  Pallas kernels  48.7 us (22%)
  starting transfers between devices  10.8 us (5%)
    all_to_all x1, blocking collectives, convolve(): lax.all_to_all(leaving, everyone, split_axis=0, concat_axis=0, tiled=True)  47.2 us
    ppermute x1, waiting for transfers between devices, convolve(): codes = lax.ppermute(codes, everyone, [(d, 127 - d) for d in range(128)])  45.9 us
    all_to_all x1, blocking collectives, convolve(): lax.all_to_all(pieces, 'row', split_axis=0, concat_axis=0, tiled=True)  32.6 us
    all_to_all x1, blocking collectives, convolve(): lax.all_to_all(convolved, 'row', split_axis=0, concat_axis=0, tiled=True)  30.6 us
    pallas_call x1, Pallas kernels, middle(): pl.pallas_call(middle_kernel, out_shape=jax.ShapeDtypeStruct((128, 88, 12...  15.4 us
    pallas_call x1, Pallas kernels, merged(): pl.pallas_call(merge_kernel, grid=(8,), out_shape=[jax.ShapeDtypeStruct((...  9.88 us
    pallas_call x1, Pallas kernels, backward(): pl.pallas_call(backward_kernel, out_shape=jax.ShapeDtypeStruct((8, 4, 264...  7.74 us
    pallas_call x1, Pallas kernels, forward(): pl.pallas_call(forward_kernel, out_shape=jax.ShapeDtypeStruct((128, 88, 1...  6.86 us
  transfers between devices with their start and end apart: 2, of which 2 were waited for; matrix products, arithmetic and copies ran while one was open for 0% of the time, Pallas kernels for 8%

profile of v6, /device:TPU:0, one launch (start us, length us, event | category | flops | bytes accessed | tf_op | source)
XLA Modules:
  0.0 220.0 jit_solution(15387078388086017538)
XLA Ops:
  0.0 6.0 %leave.1 = (bf16[8,64,16,128]{3,2,1,0:T(8,128)(2,1)}, bf16[8,3,264,128]{3,2,1,0:T(8,128)(2,1)}) custom-call(bf16[128,64,128]{2,1,0:T(8,128)(2,1)} %value_ref.1, f32[8192,128]{1,0:T(8,128)} %bitcast.6, f32[8192,128]{1,0:T(8,128)} %bitcast.8), custom_call_target="tpu_custom_call" | custom-call | flops 8000000 | bytes 14680064 | tf_op jit(solution)/shard_map/leave/pallas_call | solution.py:464
  6.0 0.0 copy-start.2
  6.0 32.6 %all_to_all.20 = bf16[8,64,16,128]{3,2,1,0:T(8,128)(2,1)S(1)} all-to-all(bf16[8,64,16,128]{3,2,1,0:T(8,128)(2,1)} %get-tuple-element.13), channel_id=1, replica_groups=mesh['row'=8,'col'=16] {'row'}, dimensions={0} | all-to-all | bytes 4194304 | tf_op jit(solution)/shard_map/all_to_all | solution.py:546
  38.6 4.6 %collective-permute-start = (bf16[8,3,264,128]{3,2,1,0:T(8,128)(2,1)}, bf16[8,3,264,128]{3,2,1,0:T(8,128)(2,1)}, u32[]{:S(2)}, u32[]{:S(2)}) collective-permute-start(bf16[8,3,264,128]{3,2,1,0:T(8,128)(2,1)} %get-tuple-element.18), channel_id=1, source_target_pairs={{0,127},{1,126},{2,125},{3,124},{4,123},{5,122},{6,121},{7,120},{8... | collective-permute-start | bytes 4866056 | tf_op jit(solution)/shard_map/ppermute | solution.py:548
  43.2 0.1 iota.47
  43.3 0.0 copy-done.2
  43.3 6.9 %forward_columns.1 = bf16[128,88,128]{2,1,0:T(8,128)(2,1)} custom-call(bf16[512,16,128]{2,1,0:T(8,128)(2,1)S(1)} %bitcast.4, f32[2048]{0:T(1024)S(1)} %copy-done.2), custom_call_target="tpu_custom_call" | custom-call | tf_op jit(solution)/shard_map/forward_columns/pallas_call | solution.py:451
  50.2 6.2 %all-to-all-start.1 = ((bf16[128,88,128]{2,1,0:T(8,128)(2,1)}), bf16[128,88,128]{2,1,0:T(8,128)(2,1)}, u32[]{:S(2)}, u32[]{:S(2)}) async-start(bf16[128,88,128]{2,1,0:T(8,128)(2,1)} %forward_columns.1), calls=%async_computation.1 | async-start | bytes 5767168 | tf_op jit(solution)/shard_map/all_to_all | solution.py:552
  56.4 0.2 add_multiply_fusion
  56.6 0.1 reshape.63
  56.7 0.2 fusion.1
  56.9 0.1 sine_select_fusion.far_ref
  57.0 0.0 copy-start.4
  57.0 45.9 %collective-permute-done.code_ref = bf16[8,3,264,128]{3,2,1,0:T(8,128)(2,1)} collective-permute-done((bf16[8,3,264,128]{3,2,1,0:T(8,128)(2,1)}, bf16[8,3,264,128]{3,2,1,0:T(8,128)(2,1)}, u32[]{:S(2)}, u32[]{:S(2)}) %collective-permute-start) | collective-permute-done | bytes 1622048 | tf_op jit(solution)/shard_map/ppermute | solution.py:548
  102.9 9.9 %merge_filters.1 = (f32[8192,128]{1,0:T(8,128)}, f32[8192,128]{1,0:T(8,128)}) custom-call(f32[8192,128]{1,0:T(8,128)} %bitcast.7, f32[8192,128]{1,0:T(8,128)} %bitcast.9, bf16[8,3,264,128]{3,2,1,0:T(8,128)(2,1)} %collective-permute-done.code_ref), custom_call_target="tpu_custom_call" | custom-call | flops 80000000000 | bytes 18874368 | tf_op jit(solution)/shard_map/merge_filters/pallas_call | solution.py:480
  112.7 3.1 %all-to-all-done.1.x_ref = bf16[128,88,128]{2,1,0:T(8,128)(2,1)} async-done(((bf16[128,88,128]{2,1,0:T(8,128)(2,1)}), bf16[128,88,128]{2,1,0:T(8,128)(2,1)}, u32[]{:S(2)}, u32[]{:S(2)}) %all-to-all-start.1) | async-done | bytes 2883616 | tf_op jit(solution)/shard_map/all_to_all | solution.py:552
  115.9 0.0 copy-done.4
  115.9 0.3 jit_solution_.3.root_ref
  116.2 15.4 %filter_rows.1 = bf16[128,88,128]{2,1,0:T(8,128)(2,1)S(1)} custom-call(bf16[128,88,128]{2,1,0:T(8,128)(2,1)} %all-to-all-done.1.x_ref, f32[2048]{0:T(1024)S(1)} %sine_select_fusion.far_ref, f32[2,8,8,128]{3,2,1,0:T(8,128)S(1)} %pad_maximum_fusion.near_ref, f32[8192,128]{1,0:T(8,128)} %get-tuple-element.19.filter_real, ...), custom_call_target="tpu_custom_call" | custom-call | tf_op jit(solution)/shard_map/filter_rows/pallas_call | solution.py:494
  131.7 47.2 %all_to_all.21.x_ref = bf16[128,88,128]{2,1,0:T(8,128)(2,1)S(1)} all-to-all(bf16[128,88,128]{2,1,0:T(8,128)(2,1)S(1)} %filter_rows.1), channel_id=1, replica_groups=mesh['row'=8,'col'=16] {'row','col'}, dimensions={0} | all-to-all | bytes 5767168 | tf_op jit(solution)/shard_map/all_to_all | solution.py:555
  178.9 7.7 %backward_columns.1 = bf16[8,4,264,128]{3,2,1,0:T(8,128)(2,1)S(1)} custom-call(bf16[128,88,128]{2,1,0:T(8,128)(2,1)S(1)} %all_to_all.21.x_ref, f32[2048]{0:T(1024)S(1)} %copy-done.2), custom_call_target="tpu_custom_call" | custom-call | tf_op jit(solution)/shard_map/backward_columns/pallas_call | solution.py:510
  186.6 0.0 copy-start
  186.7 0.0 copy-start.1
  186.7 0.0 copy-start.3
  186.7 30.6 %all_to_all.22.x_ref = bf16[8,4,264,128]{3,2,1,0:T(8,128)(2,1)S(1)} all-to-all(bf16[8,4,264,128]{3,2,1,0:T(8,128)(2,1)S(1)} %backward_columns.1), channel_id=1, replica_groups=mesh['row'=8,'col'=16] {'row'}, dimensions={0} | all-to-all | bytes 4325376 | tf_op jit(solution)/shard_map/all_to_all | solution.py:557
  217.3 0.0 copy-done
  217.3 0.0 copy-done.1
  217.3 0.0 copy-done.3
  217.3 2.8 %gating.1 = bf16[128,64,128]{2,1,0:T(8,128)(2,1)} custom-call(bf16[8,4,264,128]{3,2,1,0:T(8,128)(2,1)S(1)} %all_to_all.22.x_ref, bf16[128,64,128]{2,1,0:T(8,128)(2,1)S(1)} %copy-done, bf16[128,64,128]{2,1,0:T(8,128)(2,1)S(1)} %copy-done.1, f32[1,128]{1,0:T(1,128)S(1)} %bitcast.5), custom_call_target="tpu_custom_call" | custom-call | tf_op jit(solution)/shard_map/gating/pallas_call | solution.py:523
  (9 shorter events, 0.1 us)
Async XLA Ops:
  6.0 37.3 %copy-start.2 = (f32[2048]{0:T(1024)S(1)}, f32[2048]{0:T(1024)}, u32[]{:S(2)}) copy-start(f32[2048]{0:T(1024)} %constant.73.clone.table_ref) | copy-start | bytes 24580
  38.6 64.3 %collective-permute-start = (bf16[8,3,264,128]{3,2,1,0:T(8,128)(2,1)}, bf16[8,3,264,128]{3,2,1,0:T(8,128)(2,1)}, u32[]{:S(2)}, u32[]{:S(2)}) collective-permute-start(bf16[8,3,264,128]{3,2,1,0:T(8,128)(2,1)} %get-tuple-element.18), channel_id=1, source_target_pairs={{0,127},{1,126},{2,125},{3,124},{4,123},{5,122},{6,121},{7,120},{8... | collective-permute-start | bytes 4866056 | tf_op jit(solution)/shard_map/ppermute | solution.py:548
  50.2 65.7 %all-to-all-start.1 = ((bf16[128,88,128]{2,1,0:T(8,128)(2,1)}), bf16[128,88,128]{2,1,0:T(8,128)(2,1)}, u32[]{:S(2)}, u32[]{:S(2)}) async-start(bf16[128,88,128]{2,1,0:T(8,128)(2,1)} %forward_columns.1), calls=%async_computation.1 | async-start | bytes 5767168 | tf_op jit(solution)/shard_map/all_to_all | solution.py:552
  57.0 58.9 %copy-start.4 = (f32[2,16,8,8]{3,2,1,0:T(8,128)S(1)}, f32[2,16,8,8]{3,2,1,0:T(8,128)}, u32[]{:S(2)}) copy-start(f32[2,16,8,8]{3,2,1,0:T(8,128)} %constant.74.clone) | copy-start | bytes 24580
  186.6 30.6 %copy-start = (bf16[128,64,128]{2,1,0:T(8,128)(2,1)S(1)}, bf16[128,64,128]{2,1,0:T(8,128)(2,1)}, u32[]{:S(2)}) copy-start(bf16[128,64,128]{2,1,0:T(8,128)(2,1)} %value_ref.1) | copy-start | bytes 6291460
  186.7 30.6 %copy-start.1 = (bf16[128,64,128]{2,1,0:T(8,128)(2,1)S(1)}, bf16[128,64,128]{2,1,0:T(8,128)(2,1)}, u32[]{:S(2)}) copy-start(bf16[128,64,128]{2,1,0:T(8,128)(2,1)} %gate_ref.1) | copy-start | bytes 6291460
  186.7 30.6 %copy-start.3 = (f32[128]{0:T(128)S(1)}, f32[128]{0:T(128)}, u32[]{:S(2)}) copy-start(f32[128]{0:T(128)} %param.11) | copy-start | bytes 1540

commit v7 on v6

--- a/solution.py
+++ b/solution.py
@@ -263,8 +263,8 @@
         out_im[here, :] = im_ref[here, :] - far_im[there, :]
 
 
-def middle_kernel(x_ref, far_ref, near_ref, filter_real, filter_imag, root_ref, out_hbm,
-                  re_ref, im_ref, re2_ref, im2_ref, tc_ref, ts_ref, fr_ref, fi_ref, out_ref, sems, out_sems):
+def middle_kernel(x_ref, far_ref, near_ref, filter_real, filter_imag, root_ref, out_ref,
+                  re_ref, im_ref, re2_ref, im2_ref, tc_ref, ts_ref, fr_ref, fi_ref, sems):
     copies = [
         pltpu.make_async_copy(filter_real, fr_ref, sems.at[0]),
         pltpu.make_async_copy(filter_imag, fi_ref, sems.at[1]),
@@ -331,10 +331,10 @@
 
         encode(blocks, store)
 
-    send_parts(fifth, 128, TE, out_ref, out_hbm, out_sems)
-
-
-def backward_kernel(x_ref, table_ref, out_hbm, re_ref, im_ref, conv_ref, out_ref, sems):
+    repeat(128, fifth, TE)
+
+
+def backward_kernel(x_ref, table_ref, out_ref, re_ref, im_ref, conv_ref):
     def first(d):
         scale = decode_scale(x_ref[d, 80:88, :])
         for i in range(5):
@@ -381,7 +381,7 @@
 
         encode(blocks, store)
 
-    send_parts(fourth, 32, 8, out_ref, out_hbm, sems)
+    repeat(32, fourth, 8)
 
 
 def gate_kernel(x_ref, value_ref, gate_ref, skip_ref, out_ref):
@@ -495,12 +495,11 @@
         middle_kernel,
         out_shape=jax.ShapeDtypeStruct((128, 88, 128), bf16),
         in_specs=[vspec(), sspec(), vspec(), aspec(), aspec(), vspec()],
-        out_specs=aspec(),
+        out_specs=vspec(),
         scratch_shapes=[pltpu.VMEM((5 * STR, 128), f32)] * 4
         + [pltpu.VMEM((128, 5, 8, 128), f32)] * 2
         + [pltpu.VMEM((8192, 128), f32)] * 2
-        + [pltpu.VMEM((128, 88, 128), bf16)]
-        + [pltpu.SemaphoreType.DMA((2,)), pltpu.SemaphoreType.DMA((4,))],
+        + [pltpu.SemaphoreType.DMA((2,))],
         compiler_params=params(50),
         name="filter_rows",
     )(arrived, far, near, filter_real, filter_imag, roots)
@@ -511,9 +510,8 @@
         backward_kernel,
         out_shape=jax.ShapeDtypeStruct((8, 4, 264, 128), bf16),
         in_specs=[vspec(), sspec()],
-        out_specs=aspec(),
-        scratch_shapes=[pltpu.VMEM((5 * STR, 128), f32)] * 2 + [pltpu.VMEM((8, 128, 8, 128), f32)]
-        + [pltpu.VMEM((8, 4, 264, 128), bf16), pltpu.SemaphoreType.DMA((4,))],
+        out_specs=vspec(),
+        scratch_shapes=[pltpu.VMEM((5 * STR, 128), f32)] * 2 + [pltpu.VMEM((8, 128, 8, 128), f32)],
         compiler_params=params(24),
         name="backward_columns",
     )(returned, table)

time: 221 us -> 219 us (level)
  no operation moved by 1% of the time
where the time goes in v7:
time: 219 us
  blocking collectives  110 us (50%)
  waiting for transfers between devices  49 us (22%)
  Pallas kernels  47.2 us (22%)
  starting transfers between devices  10.8 us (5%)
    all_to_all x1, blocking collectives, convolve(): lax.all_to_all(leaving, everyone, split_axis=0, concat_axis=0, tiled=True)  47.2 us
    ppermute x1, waiting for transfers between devices, convolve(): codes = lax.ppermute(codes, everyone, [(d, 127 - d) for d in range(128)])  45.9 us
    all_to_all x1, blocking collectives, convolve(): lax.all_to_all(pieces, 'row', split_axis=0, concat_axis=0, tiled=True)  32.6 us
    all_to_all x1, blocking collectives, convolve(): lax.all_to_all(convolved, 'row', split_axis=0, concat_axis=0, tiled=True)  30.6 us
    pallas_call x1, Pallas kernels, middle(): pl.pallas_call(middle_kernel, out_shape=jax.ShapeDtypeStruct((128, 88, 12...  14.2 us
    pallas_call x1, Pallas kernels, merged(): pl.pallas_call(merge_kernel, grid=(8,), out_shape=[jax.ShapeDtypeStruct((...  9.88 us
    pallas_call x1, Pallas kernels, backward(): pl.pallas_call(backward_kernel, out_shape=jax.ShapeDtypeStruct((8, 4, 264...  7.44 us
    pallas_call x1, Pallas kernels, forward(): pl.pallas_call(forward_kernel, out_shape=jax.ShapeDtypeStruct((128, 88, 1...  6.86 us
  transfers between devices with their start and end apart: 2, of which 2 were waited for; matrix products, arithmetic and copies ran while one was open for 0% of the time, Pallas kernels for 8%

profile of v7, /device:TPU:0, one launch (start us, length us, event | category | flops | bytes accessed | tf_op | source)
XLA Modules:
  0.0 218.5 jit_solution(11432949973967123679)
XLA Ops:
  0.0 6.0 %leave.1 = (bf16[8,64,16,128]{3,2,1,0:T(8,128)(2,1)}, bf16[8,3,264,128]{3,2,1,0:T(8,128)(2,1)}) custom-call(bf16[128,64,128]{2,1,0:T(8,128)(2,1)} %value_ref.1, f32[8192,128]{1,0:T(8,128)} %bitcast.6, f32[8192,128]{1,0:T(8,128)} %bitcast.8), custom_call_target="tpu_custom_call" | custom-call | flops 8000000 | bytes 14680064 | tf_op jit(solution)/shard_map/leave/pallas_call | solution.py:464
  6.0 0.0 copy-start.2
  6.0 32.6 %all_to_all.20 = bf16[8,64,16,128]{3,2,1,0:T(8,128)(2,1)S(1)} all-to-all(bf16[8,64,16,128]{3,2,1,0:T(8,128)(2,1)} %get-tuple-element.13), channel_id=1, replica_groups=mesh['row'=8,'col'=16] {'row'}, dimensions={0} | all-to-all | bytes 4194304 | tf_op jit(solution)/shard_map/all_to_all | solution.py:544
  38.6 4.6 %collective-permute-start = (bf16[8,3,264,128]{3,2,1,0:T(8,128)(2,1)}, bf16[8,3,264,128]{3,2,1,0:T(8,128)(2,1)}, u32[]{:S(2)}, u32[]{:S(2)}) collective-permute-start(bf16[8,3,264,128]{3,2,1,0:T(8,128)(2,1)} %get-tuple-element.18), channel_id=1, source_target_pairs={{0,127},{1,126},{2,125},{3,124},{4,123},{5,122},{6,121},{7,120},{8... | collective-permute-start | bytes 4866056 | tf_op jit(solution)/shard_map/ppermute | solution.py:546
  43.2 0.1 iota.47
  43.3 0.0 copy-done.2
  43.3 6.9 %forward_columns.1 = bf16[128,88,128]{2,1,0:T(8,128)(2,1)} custom-call(bf16[512,16,128]{2,1,0:T(8,128)(2,1)S(1)} %bitcast.4, f32[2048]{0:T(1024)S(1)} %copy-done.2), custom_call_target="tpu_custom_call" | custom-call | tf_op jit(solution)/shard_map/forward_columns/pallas_call | solution.py:451
  50.2 6.2 %all-to-all-start.1 = ((bf16[128,88,128]{2,1,0:T(8,128)(2,1)}), bf16[128,88,128]{2,1,0:T(8,128)(2,1)}, u32[]{:S(2)}, u32[]{:S(2)}) async-start(bf16[128,88,128]{2,1,0:T(8,128)(2,1)} %forward_columns.1), calls=%async_computation.1 | async-start | bytes 5767168 | tf_op jit(solution)/shard_map/all_to_all | solution.py:550
  56.4 0.2 add_multiply_fusion
  56.6 0.1 reshape.63
  56.7 0.2 fusion.1
  56.9 0.1 sine_select_fusion.far_ref
  57.0 0.0 copy-start.4
  57.0 45.9 %collective-permute-done.code_ref = bf16[8,3,264,128]{3,2,1,0:T(8,128)(2,1)} collective-permute-done((bf16[8,3,264,128]{3,2,1,0:T(8,128)(2,1)}, bf16[8,3,264,128]{3,2,1,0:T(8,128)(2,1)}, u32[]{:S(2)}, u32[]{:S(2)}) %collective-permute-start) | collective-permute-done | bytes 1622048 | tf_op jit(solution)/shard_map/ppermute | solution.py:546
  102.9 9.9 %merge_filters.1 = (f32[8192,128]{1,0:T(8,128)}, f32[8192,128]{1,0:T(8,128)}) custom-call(f32[8192,128]{1,0:T(8,128)} %bitcast.7, f32[8192,128]{1,0:T(8,128)} %bitcast.9, bf16[8,3,264,128]{3,2,1,0:T(8,128)(2,1)} %collective-permute-done.code_ref), custom_call_target="tpu_custom_call" | custom-call | flops 80000000000 | bytes 18874368 | tf_op jit(solution)/shard_map/merge_filters/pallas_call | solution.py:480
  112.7 3.1 %all-to-all-done.1.x_ref = bf16[128,88,128]{2,1,0:T(8,128)(2,1)} async-done(((bf16[128,88,128]{2,1,0:T(8,128)(2,1)}), bf16[128,88,128]{2,1,0:T(8,128)(2,1)}, u32[]{:S(2)}, u32[]{:S(2)}) %all-to-all-start.1) | async-done | bytes 2883616 | tf_op jit(solution)/shard_map/all_to_all | solution.py:550
  115.9 0.0 copy-done.4
  115.9 0.3 jit_solution_.3.root_ref
  116.2 14.2 %filter_rows.1 = bf16[128,88,128]{2,1,0:T(8,128)(2,1)S(1)} custom-call(bf16[128,88,128]{2,1,0:T(8,128)(2,1)} %all-to-all-done.1.x_ref, f32[2048]{0:T(1024)S(1)} %sine_select_fusion.far_ref, f32[2,8,8,128]{3,2,1,0:T(8,128)S(1)} %pad_maximum_fusion.near_ref, f32[8192,128]{1,0:T(8,128)} %get-tuple-element.19.filter_real, ...), custom_call_target="tpu_custom_call" | custom-call | tf_op jit(solution)/shard_map/filter_rows/pallas_call | solution.py:494
  130.5 47.2 %all_to_all.21.x_ref = bf16[128,88,128]{2,1,0:T(8,128)(2,1)S(1)} all-to-all(bf16[128,88,128]{2,1,0:T(8,128)(2,1)S(1)} %filter_rows.1), channel_id=1, replica_groups=mesh['row'=8,'col'=16] {'row','col'}, dimensions={0} | all-to-all | bytes 5767168 | tf_op jit(solution)/shard_map/all_to_all | solution.py:553
  177.7 7.4 %backward_columns.1 = bf16[8,4,264,128]{3,2,1,0:T(8,128)(2,1)S(1)} custom-call(bf16[128,88,128]{2,1,0:T(8,128)(2,1)S(1)} %all_to_all.21.x_ref, f32[2048]{0:T(1024)S(1)} %copy-done.2), custom_call_target="tpu_custom_call" | custom-call | tf_op jit(solution)/shard_map/backward_columns/pallas_call | solution.py:509
  185.1 0.0 copy-start
  185.2 0.0 copy-start.1
  185.2 0.0 copy-start.3
  185.2 30.6 %all_to_all.22.x_ref = bf16[8,4,264,128]{3,2,1,0:T(8,128)(2,1)S(1)} all-to-all(bf16[8,4,264,128]{3,2,1,0:T(8,128)(2,1)S(1)} %backward_columns.1), channel_id=1, replica_groups=mesh['row'=8,'col'=16] {'row'}, dimensions={0} | all-to-all | bytes 4325376 | tf_op jit(solution)/shard_map/all_to_all | solution.py:555
  215.8 0.0 copy-done
  215.8 0.0 copy-done.1
  215.8 0.0 copy-done.3
  215.8 2.8 %gating.1 = bf16[128,64,128]{2,1,0:T(8,128)(2,1)} custom-call(bf16[8,4,264,128]{3,2,1,0:T(8,128)(2,1)S(1)} %all_to_all.22.x_ref, bf16[128,64,128]{2,1,0:T(8,128)(2,1)S(1)} %copy-done, bf16[128,64,128]{2,1,0:T(8,128)(2,1)S(1)} %copy-done.1, f32[1,128]{1,0:T(1,128)S(1)} %bitcast.5), custom_call_target="tpu_custom_call" | custom-call | tf_op jit(solution)/shard_map/gating/pallas_call | solution.py:521
  (9 shorter events, 0.1 us)
Async XLA Ops:
  6.0 37.3 %copy-start.2 = (f32[2048]{0:T(1024)S(1)}, f32[2048]{0:T(1024)}, u32[]{:S(2)}) copy-start(f32[2048]{0:T(1024)} %constant.73.clone.table_ref) | copy-start | bytes 24580
  38.6 64.3 %collective-permute-start = (bf16[8,3,264,128]{3,2,1,0:T(8,128)(2,1)}, bf16[8,3,264,128]{3,2,1,0:T(8,128)(2,1)}, u32[]{:S(2)}, u32[]{:S(2)}) collective-permute-start(bf16[8,3,264,128]{3,2,1,0:T(8,128)(2,1)} %get-tuple-element.18), channel_id=1, source_target_pairs={{0,127},{1,126},{2,125},{3,124},{4,123},{5,122},{6,121},{7,120},{8... | collective-permute-start | bytes 4866056 | tf_op jit(solution)/shard_map/ppermute | solution.py:546
  50.2 65.7 %all-to-all-start.1 = ((bf16[128,88,128]{2,1,0:T(8,128)(2,1)}), bf16[128,88,128]{2,1,0:T(8,128)(2,1)}, u32[]{:S(2)}, u32[]{:S(2)}) async-start(bf16[128,88,128]{2,1,0:T(8,128)(2,1)} %forward_columns.1), calls=%async_computation.1 | async-start | bytes 5767168 | tf_op jit(solution)/shard_map/all_to_all | solution.py:550
  57.0 58.9 %copy-start.4 = (f32[2,16,8,8]{3,2,1,0:T(8,128)S(1)}, f32[2,16,8,8]{3,2,1,0:T(8,128)}, u32[]{:S(2)}) copy-start(f32[2,16,8,8]{3,2,1,0:T(8,128)} %constant.74.clone) | copy-start | bytes 24580
  185.1 30.6 %copy-start = (bf16[128,64,128]{2,1,0:T(8,128)(2,1)S(1)}, bf16[128,64,128]{2,1,0:T(8,128)(2,1)}, u32[]{:S(2)}) copy-start(bf16[128,64,128]{2,1,0:T(8,128)(2,1)} %value_ref.1) | copy-start | bytes 6291460
  185.2 30.6 %copy-start.1 = (bf16[128,64,128]{2,1,0:T(8,128)(2,1)S(1)}, bf16[128,64,128]{2,1,0:T(8,128)(2,1)}, u32[]{:S(2)}) copy-start(bf16[128,64,128]{2,1,0:T(8,128)(2,1)} %gate_ref.1) | copy-start | bytes 6291460
  185.2 30.6 %copy-start.3 = (f32[128]{0:T(128)S(1)}, f32[128]{0:T(128)}, u32[]{:S(2)}) copy-start(f32[128]{0:T(128)} %param.11) | copy-start | bytes 1540
